TPU v7x, 512 devices: a whole 4x4x16 slice. The times are simulated.
512 devices in a mesh: lat: 16 (over x_hi, y, core), lon: 32 (over z, x_lo).
Axes of the slice: x: 4 (x_hi: 2, x_lo: 2; x = x_hi * 2 + x_lo), y: 4, z: 16, core: 2. Of those that a mesh axis runs over, the one named last changes fastest.
Arguments:
- fields: bfloat16 [32, 256, 8192], P('lon', 'lat'), may hold values from -6 to 6
- weight: bfloat16 [64, 32, 3, 3], replicated, may hold values from -0.375 to 0.375
- bias: float32 [64], replicated, may hold values from -3 to 3
- land_bias: float32 [64], replicated, may hold values from -4 to 4
- land_mask: int32 [256, 8192], P('lat', 'lon'), may hold values 0 or 1
- cotangent: bfloat16 [64, 128, 4096], P(None, 'lat', 'lon'), may hold values from -6 to 6
Outputs:
- pooled: bfloat16 [64, 128, 4096], P(None, 'lat', 'lon')
- grad_weight: float32 [64, 32, 3, 3], replicated
- grad_bias: float32 [64], replicated
- grad_land: float32 [64], replicated
All inputs are finite; a program needn't handle non-finite values. No bound on the sum of `land_mask` on one device may be relied on, other than what follows from the above.
Results may differ from a plain program's by a relative error of at most 0.0029.
Values may be sent and summed in bfloat16 or wider, within the bound.
No kernel may reach another device: no remote copies, remote signals or barrier semaphores. Data moves between devices by JAX's collectives and lax.ppermute only.
A program may use at most 64 MiB of HBM per device.

v0:
```python
import math

import jax
import jax.numpy as jnp
from jax import lax
from jax.sharding import PartitionSpec as P


def padded_2(block, sides, width, periodic):
    for axis, dim in sides:
        count = lax.axis_size(axis)
        forward = [(i, i + 1) for i in range(count - 1)]
        if periodic:
            forward.append((count - 1, 0))
        backward = [(target, source) for source, target in forward]
        low = lax.ppermute(
            lax.slice_in_dim(block, block.shape[dim] - width, None, axis=dim), axis, forward
        )
        high = lax.ppermute(lax.slice_in_dim(block, 0, width, axis=dim), axis, backward)
        block = jnp.concatenate([low, block, high], axis=dim)
    return block


def local(fields, weight, bias, land_bias, land_mask, cotangent):
    tiled = lax.all_to_all(fields, "lon", split_axis=2, concat_axis=0, tiled=True)
    lon_padded = padded_2(tiled, (("lon", 2),), 1, True)
    padded = padded_2(lon_padded, (("lat", 1),), 1, False)
    row_count = padded.shape[1] - 2
    col_count = padded.shape[2] - 2
    channels = weight.shape[0]
    land_float = land_mask.astype(jnp.float32)
    preact = bias[:, None, None] + land_bias[:, None, None] * land_float[None]
    for row_off in range(3):
        for col_off in range(3):
            window = padded[:, row_off : row_off + row_count, col_off : col_off + col_count]
            preact = preact + jnp.einsum(
                "oc,chw->ohw",
                weight[:, :, row_off, col_off],
                window,
                preferred_element_type=jnp.float32,
            )
    activated, pullback = jax.vjp(jax.nn.gelu, preact)
    pooled = (
        activated.reshape(channels, row_count // 2, 2, col_count // 2, 2).sum(axis=(2, 4)) * 0.25
    ).astype(jnp.bfloat16)
    total_cells = (
        cotangent.shape[1] * lax.axis_size("lat") * cotangent.shape[2] * lax.axis_size("lon")
    )
    scale = 1.0 / math.sqrt(float(total_cells))
    scaled = cotangent.astype(jnp.float32) * (scale * 0.25)
    grad_act = jnp.repeat(jnp.repeat(scaled, 2, axis=1), 2, axis=2)
    grad_pre = pullback(grad_act)[0]
    grad_low = grad_pre.astype(jnp.bfloat16)
    pieces = []
    for row_off in range(3):
        across = []
        for col_off in range(3):
            window = padded[:, row_off : row_off + row_count, col_off : col_off + col_count]
            across.append(
                jnp.einsum("ohw,chw->oc", grad_low, window, preferred_element_type=jnp.float32)
            )
        pieces.append(jnp.stack(across, axis=-1))
    local_weight = jnp.stack(pieces, axis=-2)
    local_bias = grad_pre.sum(axis=(1, 2))
    local_land = (grad_pre * land_float[None]).sum(axis=(1, 2))
    grad_weight, grad_bias, grad_land = lax.psum(
        (local_weight, local_bias, local_land), ("lat", "lon")
    )
    return (pooled, grad_weight, grad_bias, grad_land)


def solution(mesh):
    placed = (P("lon", "lat", None), P(), P(), P(), P("lat", "lon"), P(None, "lat", "lon"))
    return jax.shard_map(
        local,
        mesh=mesh,
        in_specs=placed,
        out_specs=(P(None, "lat", "lon"), P(), P(), P()),
        check_vma=False,
    )
```

profile of v0, /device:TPU:1, one launch (start us, length us, event | category | flops | bytes accessed | tf_op | source)
XLA Modules:
  0.0 600.3 jit_solution(5072349520279552494)
XLA Ops:
  7.2 8.4 %copy.15 = bf16[1,16,8192]{1,0,2:T(2,128)(2,1)} copy(bf16[1,16,8192]{2,1,0:T(8,128)(2,1)} %param.6) | data formatting | bytes 524288 | tf_op args[0]
  15.5 0.5 broadcast.32
  16.0 45.2 %reduce = bf16[8192,16]{1,0:T(8,128)(2,1)S(1)} reduce(bf16[8192,1,16]{2,1,0:T(2,128)(2,1)} %bitcast.128, bf16[]{:T(256)} %broadcast.32), dimensions={1}, to_apply=%bitcast.110.reduce_sub_computation | reduce | bytes 524290
  61.3 2.9 reshape.41
  64.1 17.0 %all-to-all-start = ((bf16[32,2,2048]{2,1,0:T(2,128)(2,1)}), bf16[32,2,2048]{2,1,0:T(2,128)(2,1)S(1)}, u32[]{:S(2)}, u32[]{:S(2)}) async-start(bf16[32,2,2048]{2,1,0:T(2,128)(2,1)} %reshape.41), calls=%async_computation | async-start | bytes 524288 | tf_op jit(solution)/shard_map/all_to_all | solution.py:25
  81.1 0.0 all-reduce.3.cloned.1.call-start
  81.2 0.3 copy.18
  81.5 0.4 broadcast_in_dim.4
  81.8 0.2 broadcast_in_dim.5
  82.0 1.0 copy.19
  83.1 18.6 %all-to-all-done = bf16[32,2,2048]{2,1,0:T(2,128)(2,1)S(1)} async-done(((bf16[32,2,2048]{2,1,0:T(2,128)(2,1)}), bf16[32,2,2048]{2,1,0:T(2,128)(2,1)S(1)}, u32[]{:S(2)}, u32[]{:S(2)}) %all-to-all-start) | async-done | bytes 262176 | tf_op jit(solution)/shard_map/all_to_all | solution.py:25
  101.6 7.6 %reshape.42 = bf16[8192,1,16]{2,1,0:T(2,128)(2,1)} reshape(bf16[32,2,2048]{2,1,0:T(2,128)(2,1)S(1)} %all-to-all-done) | data formatting | bytes 524288
  109.2 7.9 %copy.16 = bf16[1,16,8192]{2,1,0:T(8,128)(2,1)S(1)} copy(bf16[1,16,8192]{1,0,2:T(2,128)(2,1)} %bitcast.129) | data formatting | bytes 524288 | tf_op jit(solution)/shard_map/all_to_all | solution.py:25
  117.2 0.1 fusion.60
  117.3 2.0 collective-permute-start
  119.3 5.4 collective-permute-start.1
  124.7 0.3 fusion.39
  125.1 0.2 collective-permute-done
  125.3 1.6 collective-permute-done.1
  126.9 0.1 pad_maximum_fusion.10
  127.0 6.3 %collective-permute-start.2 = (bf16[32,1,258]{2,0,1:T(8,128)(2,1)S(1)}, bf16[32,1,258]{2,0,1:T(8,128)(2,1)S(1)}, u32[]{:S(2)}, u32[]{:S(2)}) collective-permute-start(bf16[32,1,258]{2,0,1:T(8,128)(2,1)S(1)} %get-tuple-element.16), channel_id=1, source_target_pairs={{0,32},{32,64},{64,96},{96,128},{128,160},{160,192},{192,224},{224... | collective-permute-start | bytes 49544 | tf_op jit(solution)/shard_map/ppermute | solution.py:16
  133.3 2.1 collective-permute-start.3
  135.4 0.4 convolution_bitcast_fusion.3
  135.8 0.4 convolution_bitcast_fusion.4
  136.2 2.3 collective-permute-done.3
  138.4 0.4 maximum_maximum_fusion
  138.8 0.4 convolution_bitcast_fusion.5
  139.2 0.4 convolution_bitcast_fusion.6
  139.6 0.4 convolution_bitcast_fusion
  140.0 0.4 convolution_bitcast_fusion.1
  140.4 0.3 convolution_bitcast_fusion.2
  140.7 2.6 multiply_reduce_fusion
  143.3 0.3 fusion.18
  143.6 0.3 fusion.21
  143.9 0.3 fusion.15
  144.2 0.3 fusion.24
  144.6 0.3 fusion.27
  144.9 0.3 fusion.30
  145.2 0.3 fusion.54
  145.4 0.3 fusion.34
  145.8 0.3 fusion.33
  146.1 0.7 pad_maximum_fusion.3
  146.8 0.6 copy.17
  147.4 1.7 reduce_sum.27
  149.2 0.8 copy.21
  150.0 107.5 %all-reduce = (f32[64]{0:T(128)}, f32[64]{0:T(128)}) all-reduce(f32[64]{0:T(128)S(1)} %get-tuple-element.9, f32[64]{0:T(128)S(1)} %get-tuple-element.8), channel_id=1, replica_groups=mesh['lat'=16,'lon'=32] {'lat','lon'}, use_global_device_ids=true, to_apply=%region_3.0 | all-reduce | flops 128 | bytes 1024 | tf_op jit(solution)/shard_map/psum | solution.py:66
  257.5 334.4 %all-reduce.3.cloned.1.call-done = f32[64,32,3,3]{0,1,3,2:T(8,128)} async-done(((f32[64,32,3,3]{0,1,3,2:T(8,128)}), f32[64,32,3,3]{0,1,3,2:T(8,128)}) %all-reduce.3.cloned.1.call-update) | async-done | bytes 73744 | tf_op jit(solution)/shard_map/psum | solution.py:66
  591.9 1.6 copy.24
  (21 shorter events, 0.2 us)
Async XLA Ops:
  61.3 19.9 %copy-start.3 = (s32[16,256]{1,0:T(8,128)S(1)}, s32[16,256]{1,0:T(8,128)}, u32[]{:S(2)}) copy-start(s32[16,256]{1,0:T(8,128)} %param.10) | copy-start | bytes 49156
  61.3 19.9 %copy-start.1 = (bf16[64,8,128]{2,1,0:T(8,128)(2,1)S(1)}, bf16[64,8,128]{2,1,0:T(8,128)(2,1)}, u32[]{:S(2)}) copy-start(bf16[64,8,128]{2,1,0:T(8,128)(2,1)} %param.11) | copy-start | bytes 393220
  64.1 37.5 %all-to-all-start = ((bf16[32,2,2048]{2,1,0:T(2,128)(2,1)}), bf16[32,2,2048]{2,1,0:T(2,128)(2,1)S(1)}, u32[]{:S(2)}, u32[]{:S(2)}) async-start(bf16[32,2,2048]{2,1,0:T(2,128)(2,1)} %reshape.41), calls=%async_computation | async-start | bytes 524288 | tf_op jit(solution)/shard_map/all_to_all | solution.py:25
  81.1 510.8 %all-reduce.3.cloned.1.call-start = ((), (), s32[]{:S(2)}) async-start(), calls=%async_computation.1 | async-start | bytes 294912 | tf_op jit(solution)/shard_map/psum | solution.py:66
  109.2 15.5 %copy-start.2 = (bf16[64,32,3,3]{0,1,3,2:T(8,128)(2,1)S(1)}, bf16[64,32,3,3]{0,1,3,2:T(8,128)(2,1)}, u32[]{:S(2)}) copy-start(bf16[64,32,3,3]{0,1,3,2:T(8,128)(2,1)} %param.7) | copy-start | bytes 110596
  117.3 7.9 %collective-permute-start = (bf16[32,16,1]{2,0,1:T(8,128)(2,1)S(1)}, bf16[32,16,1]{2,0,1:T(8,128)(2,1)S(1)}, u32[]{:S(2)}, u32[]{:S(2)}) collective-permute-start(bf16[32,16,1]{2,0,1:T(8,128)(2,1)S(1)} %get-tuple-element.18), channel_id=1, source_target_pairs={{0,1},{1,2},{2,3},{3,4},{4,5},{5,6},{6,7},{7,8},{8,9},{9,10},{10,1... | collective-permute-start | bytes 3080 | tf_op jit(solution)/shard_map/ppermute | solution.py:16
  119.3 7.5 %collective-permute-start.1 = (bf16[32,16,1]{2,0,1:T(8,128)(2,1)S(1)}, bf16[32,16,1]{2,0,1:T(8,128)(2,1)S(1)}, u32[]{:S(2)}, u32[]{:S(2)}) collective-permute-start(bf16[32,16,1]{2,0,1:T(8,128)(2,1)S(1)} %get-tuple-element.19), channel_id=1, source_target_pairs={{1,0},{2,1},{3,2},{4,3},{5,4},{6,5},{7,6},{8,7},{9,8},{10,9},{11,1... | collective-permute-start | bytes 3080 | tf_op jit(solution)/shard_map/ppermute | solution.py:19
  127.0 9.2 %collective-permute-start.2 = (bf16[32,1,258]{2,0,1:T(8,128)(2,1)S(1)}, bf16[32,1,258]{2,0,1:T(8,128)(2,1)S(1)}, u32[]{:S(2)}, u32[]{:S(2)}) collective-permute-start(bf16[32,1,258]{2,0,1:T(8,128)(2,1)S(1)} %get-tuple-element.16), channel_id=1, source_target_pairs={{0,32},{32,64},{64,96},{96,128},{128,160},{160,192},{192,224},{224... | collective-permute-start | bytes 49544 | tf_op jit(solution)/shard_map/ppermute | solution.py:16
  133.3 5.1 collective-permute-start.3
  139.6 1.1 copy-start.4
  139.6 1.1 copy-start.5
  144.9 1.9 copy-start
Sparse Core Ops, SparseCore 0:
  146.9 444.8 all-reduce.2
where the time goes:
time: 602 us; the launch traced here: 600 us
  waiting for transfers between devices  357 us (59%)
  blocking collectives  107 us (18%)
  other arithmetic  48.2 us (8%)
  starting transfers between devices  32.8 us (5%)
  local copies, waits for them, and re-layouts  32.2 us (5%)
  between operations  14.3 us (2%)
  matrix products  8.22 us (1%)
    psum x1, waiting for transfers between devices, local(): lax.psum((local_weight, local_bias, local_land), ('lat', 'lon'))  334 us
    psum x1, blocking collectives, local(): lax.psum((local_weight, local_bias, local_land), ('lat', 'lon'))  107 us
    unnamed x1, other arithmetic  45.2 us
    unnamed x19, local copies, waits for them, and re-layouts  21.8 us
    all_to_all x1, waiting for transfers between devices, local(): lax.all_to_all(fields, 'lon', split_axis=2, concat_axis=0, tiled=True)  18.6 us
    all_to_all x1, starting transfers between devices, local(): lax.all_to_all(fields, 'lon', split_axis=2, concat_axis=0, tiled=True)  17 us
  transfers between devices with their start and end apart: 6, of which 5 were waited for; matrix products, arithmetic and copies ran while one was open for 1% of the time, Pallas kernels for 0%

commit v1 on v0

v1 whole, which is shorter than its diff:
```python
import functools
import math

import jax
import jax.numpy as jnp
from jax import lax
from jax.experimental import pallas as pl
from jax.experimental.pallas import tpu as pltpu
from jax.sharding import Mesh
from jax.sharding import PartitionSpec as P

AXES = ("xh", "y", "c", "z", "xl")
LAT = ("xh", "y", "c")
LON = ("z", "xl")
PLANE = ("xh", "xl", "y", "c")
F32 = jnp.float32
BF16 = jnp.bfloat16
ROWS = 16
COLS = 256
LANES = 128
PIECE = 40
VMEM = pl.BlockSpec(memory_space=pltpu.VMEM)


def iota(shape, dim):
    return lax.broadcasted_iota(jnp.int32, shape, dim)


def pack_kernel(tiles, x_ref, top_ref, bottom_ref, out_ref):
    rows8 = iota((8, LANES), 0)
    lanes = iota((24, LANES), 1)
    edges = jnp.zeros((24, LANES), F32)
    tails = []
    for tile in range(tiles):
        blocks = []
        for half in range(2):
            at = pl.ds(tile * COLS + half * LANES, LANES)
            body = x_ref[:, at]
            out_ref[tile, half * ROWS : (half + 1) * ROWS, :] = body
            top = top_ref[:, at].astype(F32)
            bottom = bottom_ref[:, at].astype(F32)
            blocks.append((top, bottom))
            halo = jnp.where(rows8 == 0, top, jnp.where(rows8 == 1, bottom, 0.0))
            block = jnp.concatenate([body.astype(F32), halo], axis=0)
            if half == 0:
                source, target = 0, 64 + (tile - 1) % tiles
            else:
                source, target = LANES - 1, (tile + 1) % tiles
            turned = pltpu.roll(block, (target - source) % LANES, 1)
            edges = jnp.where(lanes == target, turned, edges)
        tails.append(blocks)
    square = jnp.concatenate([edges, jnp.zeros((LANES - 24, LANES), F32)], axis=0).T
    columns = square[:tiles] + pltpu.roll(square[64 : 64 + tiles], 64, 1)
    for tile, ((top0, bottom0), (top1, bottom1)) in enumerate(tails):
        tail = jnp.where(rows8 == 0, top0, 0.0)
        tail = jnp.where(rows8 == 1, top1, tail)
        tail = jnp.where(rows8 == 2, bottom0, tail)
        tail = jnp.where(rows8 == 3, bottom1, tail)
        tail = jnp.where(rows8 == 4, columns[tile : tile + 1], tail)
        out_ref[tile, 2 * ROWS : PIECE, :] = tail.astype(BF16)


def column_of(row, count):
    return jnp.sum(jnp.where(iota((count, count), 0) == iota((count, count), 1), row, 0.0), axis=1, keepdims=True)


def conv_kernel(
    factor, r_ref, w_ref, bias_ref, land_ref, mask_ref, cot_ref, pooled_ref, sums_ref, flat_ref, patch_ref, wide0, wide1, act0, act1
):
    fields = r_ref.shape[0]
    channels = w_ref.shape[1]
    taps = 9 * fields
    pool_rows = ROWS // 2
    for c in range(fields):
        flat_ref[c * PIECE : (c + 1) * PIECE, :] = r_ref[c].astype(F32)

    def take(k):
        return flat_ref[pl.ds(k, fields, stride=PIECE), :]

    columns = take(36)
    col = iota((fields, COLS), 1)
    for r in range(ROWS + 2):
        if r == 0:
            first, second, lane = 32, 33, 16
        elif r == ROWS + 1:
            first, second, lane = 34, 35, 17
        else:
            first, second, lane = r - 1, ROWS + r - 1, r - 1
        x = jnp.concatenate([take(first), take(second)], axis=1)
        left = jnp.where(col == 0, columns[:, lane : lane + 1], pltpu.roll(x, 1, 1))
        right = jnp.where(col == COLS - 1, columns[:, 64 + lane : 65 + lane], pltpu.roll(x, COLS - 1, 1))
        patch_ref[r, 0:fields, :] = left.astype(BF16)
        patch_ref[r, fields : 2 * fields, :] = x.astype(BF16)
        patch_ref[r, 2 * fields : 3 * fields, :] = right.astype(BF16)

    weight = w_ref[...].astype(F32).T.astype(BF16)
    bias = column_of(bias_ref[...], channels)
    land = column_of(land_ref[...], channels)
    spread = (iota((LANES, COLS), 1) // 2 == iota((LANES, COLS), 0)).astype(F32).astype(BF16)
    wide = jnp.dot(cot_ref[...].reshape(channels * pool_rows, LANES), spread, preferred_element_type=F32) * factor
    wide0[...] = wide[:, :LANES]
    wide1[...] = wide[:, LANES:]

    root = math.sqrt(2.0 / math.pi)
    grad_w = jnp.zeros((taps, channels), F32)
    grad_b = jnp.zeros((channels, COLS), F32)
    grad_l = jnp.zeros((channels, COLS), F32)
    for p in range(pool_rows):
        here = pl.ds(p, channels, stride=pool_rows)
        grad_act = jnp.concatenate([wide0[here, :], wide1[here, :]], axis=1)
        act = None
        for i in (2 * p, 2 * p + 1):
            patch = patch_ref[i : i + 3].reshape(taps, COLS)
            mask = mask_ref[i : i + 1, :].astype(F32)
            v = jnp.dot(weight, patch, preferred_element_type=F32) + (bias + land * mask)
            square = v * v
            t = jnp.tanh(v * (root + (root * 0.044715) * square))
            half = 0.5 + 0.5 * t
            gelu = v * half
            slope = half + gelu * (1.0 - t) * (root + (3.0 * root * 0.044715) * square)
            grad_pre = grad_act * slope
            grad_w += lax.dot_general(
                patch, grad_pre.astype(BF16), (((1,), (1,)), ((), ())), preferred_element_type=F32
            )
            grad_b += grad_pre
            grad_l += grad_pre * mask
            act = gelu if act is None else act + gelu
        act0[here, :] = act[:, :LANES]
        act1[here, :] = act[:, LANES:]

    pair = (iota((COLS, LANES), 0) // 2 == iota((COLS, LANES), 1)).astype(F32).astype(BF16)
    total = jnp.concatenate([act0[...], act1[...]], axis=1)
    high = total.astype(BF16)
    low = (total - high.astype(F32)).astype(BF16)
    pooled = jnp.dot(high, pair, preferred_element_type=F32) + jnp.dot(low, pair, preferred_element_type=F32)
    pooled_ref[...] = (pooled * 0.25).astype(BF16).reshape(pooled_ref.shape)

    ones = jnp.ones((8, COLS), F32)

    def across(grad):
        return lax.dot_general(
            ones, grad, (((1,), (1,)), ((), ())), precision=lax.Precision.HIGHEST, preferred_element_type=F32
        )

    half_taps = taps // 2
    used = half_taps // 8
    sums_ref[0:used] = jnp.concatenate([grad_w[:half_taps], grad_w[half_taps:]], axis=1).reshape(used, 8, LANES)
    sums_ref[used] = jnp.concatenate([across(grad_b), across(grad_l)], axis=1)
    sums_ref[used + 1 :] = jnp.zeros((sums_ref.shape[0] - used - 1, 8, LANES), F32)


def sum_kernel(x_ref, out_ref):
    out_ref[...] = jnp.broadcast_to(jnp.sum(x_ref[...], axis=0, keepdims=True), out_ref.shape)


def unpack_kernel(x_ref, weight_ref, bias_ref, land_ref):
    half_taps = weight_ref.shape[0] // 2
    channels = weight_ref.shape[1]
    used = half_taps // 8
    both = x_ref[0:used].reshape(half_taps, LANES)
    weight_ref[0:half_taps, :] = both[:, :channels]
    weight_ref[half_taps:, :] = both[:, channels:]
    bias_ref[...] = x_ref[used, 0:1, :channels]
    land_ref[...] = x_ref[used, 0:1, channels:]


def call(kernel, name, outs, *args, scratch=(), flops=0):
    shapes = [jax.ShapeDtypeStruct(*o) for o in outs]
    single = len(shapes) == 1
    return pl.pallas_call(
        kernel,
        name=name,
        out_shape=shapes[0] if single else shapes,
        in_specs=[VMEM] * len(args),
        out_specs=VMEM if single else [VMEM] * len(shapes),
        scratch_shapes=list(scratch),
        compiler_params=pltpu.CompilerParams(vmem_limit_bytes=32 * 1024 * 1024),
    )(*args)


def local(fields, weight, bias, land_bias, land_mask, cotangent):
    channels, in_fields = weight.shape[:2]
    taps = 9 * in_fields
    tiles = lax.axis_size(LON)
    rows_count = lax.axis_size(LAT)
    field = fields[0]
    up = [(i, i + 1) for i in range(rows_count - 1)]
    down = [(i + 1, i) for i in range(rows_count - 1)]
    top = lax.ppermute(field[ROWS - 1 :], LAT, up)
    bottom = lax.ppermute(field[:1], LAT, down)
    pieces = call(
        functools.partial(pack_kernel, tiles), "pack", [((tiles, PIECE, LANES), BF16)], field, top, bottom
    )
    pieces = lax.all_to_all(pieces, LON, 0, 0, tiled=True)
    factor = 0.25 / math.sqrt(float(cotangent.shape[1] * rows_count * cotangent.shape[2] * tiles))
    members = lax.axis_size(PLANE)
    pooled, sums = call(
        functools.partial(conv_kernel, factor),
        "conv",
        [(cotangent.shape, BF16), ((members, 8, LANES), F32)],
        pieces,
        weight.transpose(2, 3, 1, 0).reshape(taps, channels),
        bias.reshape(1, channels),
        land_bias.reshape(1, channels),
        land_mask,
        cotangent,
        scratch=[
            pltpu.VMEM((in_fields * PIECE, LANES), F32),
            pltpu.VMEM((ROWS + 2, 3 * in_fields, COLS), BF16),
        ]
        + [pltpu.VMEM((channels * ROWS // 2, LANES), F32)] * 4,
    )
    sums = lax.all_to_all(sums, PLANE, 0, 0, tiled=True)
    sums = call(sum_kernel, "sum_plane", [((lax.axis_size("z"), 8, LANES), F32)], sums)
    sums = lax.all_to_all(sums, "z", 0, 0, tiled=True)
    sums = call(sum_kernel, "sum_z", [((members, 8, LANES), F32)], sums)
    sums = lax.all_to_all(sums, PLANE, 0, 0, tiled=True)
    grad_weight, grad_bias, grad_land = call(
        unpack_kernel,
        "unpack",
        [((taps, channels), F32), ((1, channels), F32), ((1, channels), F32)],
        sums,
    )
    grad_weight = grad_weight.reshape(3, 3, in_fields, channels).transpose(3, 2, 0, 1)
    return pooled, grad_weight, grad_bias.reshape(channels), grad_land.reshape(channels)


def solution(mesh):
    physical = Mesh(mesh.devices.reshape(2, 4, 2, 16, 2), AXES)
    placed = (P(LON, LAT, None), P(), P(), P(), P(LAT, LON), P(None, LAT, LON))
    return jax.shard_map(
        local,
        mesh=physical,
        in_specs=placed,
        out_specs=(P(None, LAT, LON), P(), P(), P()),
        check_vma=False,
    )
```

time: 602 us -> 97.9 us (0.16)
  waiting for transfers between devices: 357 us -> 1.17 us
  other arithmetic: 48.2 us -> 0 us
  local copies, waits for them, and re-layouts: 32.2 us -> 2.65 us
  blocking collectives: 107 us -> 78.6 us
  starting transfers between devices: 32.8 us -> 10.7 us
  between operations: 14.3 us -> 0.71 us
  matrix products: 8.22 us -> 0 us
    psum x1 -> x0, waiting for transfers between devices: 334 us -> none  [local(): lax.psum((local_weight, local_bias, local_land), ('lat', 'lon'))]
    psum x1 -> x0, blocking collectives: 107 us -> none  [local(): lax.psum((local_weight, local_bias, local_land), ('lat', 'lon'))]
    all_to_all x0 -> x4, blocking collectives: none -> 78.6 us  [the longest x1 36.9 us: local(): pieces = lax.all_to_all(pieces, LON, 0, 0, tiled=True)]
    unnamed x1 -> x0, other arithmetic: 45.2 us -> none
    unnamed x19 -> x12, local copies, waits for them, and re-layouts: 21.8 us -> 1.62 us
    all_to_all x1 -> x0, waiting for transfers between devices: 18.6 us -> none  [local(): lax.all_to_all(fields, 'lon', split_axis=2, concat_axis=0, tiled=True)]
    all_to_all x1 -> x0, starting transfers between devices: 17 us -> none  [local(): lax.all_to_all(fields, 'lon', split_axis=2, concat_axis=0, tiled=True)]
    dot_general x18 -> x0, matrix products: 8.22 us -> none  [the longest x9 5.47 us: local(): jnp.einsum('oc,chw->ohw', weight[:, :, row_off, col_off], window, preferr...]
  transfers between devices with their start and end apart: 6 -> 2, of which waited for: 5 -> 1; matrix products, arithmetic and copies ran while one was open for 1% -> 0% of each run, Pallas kernels for 0% -> 0%
where the time goes in v1:
time: 97.9 us; the launch traced here: 97.6 us
  blocking collectives  78.6 us (80%)
  starting transfers between devices  10.7 us (11%)
  Pallas kernels  3.69 us (4%)
  local copies, waits for them, and re-layouts  2.65 us (3%)
  waiting for transfers between devices  1.17 us (1%)
    all_to_all x1, blocking collectives, local(): pieces = lax.all_to_all(pieces, LON, 0, 0, tiled=True)  36.9 us
    all_to_all x2, blocking collectives, local(): sums = lax.all_to_all(sums, PLANE, 0, 0, tiled=True)  27.5 us
    all_to_all x1, blocking collectives, local(): sums = lax.all_to_all(sums, 'z', 0, 0, tiled=True)  14.3 us
    ppermute x1, starting transfers between devices, local(): bottom = lax.ppermute(field[:1], LAT, down)  8.79 us
    pallas_call x5, Pallas kernels, call(): pl.pallas_call(kernel, name=name, out_shape=shapes[0] if single else shap...  3.69 us
  transfers between devices with their start and end apart: 2, of which 1 were waited for; matrix products, arithmetic and copies ran while one was open for 0% of the time, Pallas kernels for 0%

profile of v1, /device:TPU:1, one launch (start us, length us, event | category | flops | bytes accessed | tf_op | source)
XLA Modules:
  0.0 97.6 jit_solution(3490859993735238919)
XLA Ops:
  0.6 1.0 %slice_bitcast_fusion = (bf16[1,8192]{1,0:T(2,128)(2,1)S(1)}, bf16[1,8192]{1,0:T(2,128)(2,1)S(1)}) fusion(bf16[1,16,8192]{2,1,0:T(8,128)(2,1)} %param.6), kind=kLoop, calls=%fused_computation | loop fusion | bytes 65536 | tf_op jit(solution)/shard_map/slice | solution.py:190
  1.7 8.8 %collective-permute-start.1 = (bf16[1,8192]{1,0:T(2,128)(2,1)S(1)}, bf16[1,8192]{1,0:T(2,128)(2,1)S(1)}, u32[]{:S(2)}, u32[]{:S(2)}) collective-permute-start(bf16[1,8192]{1,0:T(2,128)(2,1)S(1)} %get-tuple-element.14), channel_id=1, source_target_pairs={{32,0},{64,32},{96,64},{128,96},{160,128},{192,160},{224,192},{256... | collective-permute-start | bytes 49160 | tf_op jit(solution)/shard_map/ppermute | solution.py:190
  10.5 1.9 %collective-permute-start = (bf16[1,8192]{1,0:T(2,128)(2,1)S(1)}, bf16[1,8192]{1,0:T(2,128)(2,1)S(1)}, u32[]{:S(2)}, u32[]{:S(2)}) collective-permute-start(bf16[1,8192]{1,0:T(2,128)(2,1)S(1)} %get-tuple-element.15), channel_id=1, source_target_pairs={{0,32},{32,64},{64,96},{96,128},{128,160},{160,192},{192,224},{224... | collective-permute-start | bytes 49160 | tf_op jit(solution)/shard_map/ppermute | solution.py:189
  12.4 0.0 collective-permute-done.1.bottom_ref
  12.4 1.2 %collective-permute-done.top_ref = bf16[1,8192]{1,0:T(2,128)(2,1)S(1)} collective-permute-done((bf16[1,8192]{1,0:T(2,128)(2,1)S(1)}, bf16[1,8192]{1,0:T(2,128)(2,1)S(1)}, u32[]{:S(2)}, u32[]{:S(2)}) %collective-permute-start) | collective-permute-done | bytes 16416 | tf_op jit(solution)/shard_map/ppermute | solution.py:189
  13.6 0.0 copy-start
  13.6 0.9 copy-done
  14.5 0.4 pack.1
  14.9 0.0 copy-start.1
  14.9 0.0 copy-start.2
  14.9 0.0 copy-start.3
  14.9 36.9 %all_to_all.20.r_ref = bf16[32,40,128]{2,1,0:T(8,128)(2,1)S(1)} all-to-all(bf16[32,40,128]{2,1,0:T(8,128)(2,1)S(1)} %pack.1), channel_id=1, replica_groups=mesh['xh'=2,'y'=4,'c'=2,'z'=16,'xl'=2] {'z','xl'}, dimensions={0} | all-to-all | bytes 655360 | tf_op jit(solution)/shard_map/all_to_all | solution.py:194
  51.8 0.0 copy-start.4
  51.8 0.0 copy-start.5
  51.8 0.0 copy-done.1
  51.9 0.0 copy-done.2
  51.9 0.0 copy-done.3
  51.9 0.6 copy-done.4
  52.5 0.0 copy-done.5
  52.5 2.5 %conv.1 = (bf16[64,8,128]{2,1,0:T(8,128)(2,1)}, f32[32,8,128]{2,1,0:T(8,128)S(1)}) custom-call(bf16[32,40,128]{2,1,0:T(8,128)(2,1)S(1)} %all_to_all.20.r_ref, bf16[288,64]{1,0:T(8,128)(2,1)S(1)} %bitcast.16, f32[1,64]{1,0:T(1,128)S(1)} %bitcast.17, f32[1,64]{1,0:T(1,128)S(1)} %bitcast.18, s32[16,256]{1,0:T(8,128)S(1)} %copy-done.3, ...), custom_call_target="tpu_custom_call" | custom-call | tf_op jit(solution)/shard_map/conv/pallas_call | solution.py:170
  55.0 14.7 %all_to_all.21.x_ref = f32[32,8,128]{2,1,0:T(8,128)S(1)} all-to-all(f32[32,8,128]{2,1,0:T(8,128)S(1)} %get-tuple-element.10), channel_id=1, replica_groups=mesh['xh'=2,'y'=4,'c'=2,'z'=16,'xl'=2] {'xh','xl','y','c'}, dimensions={0} | all-to-all | bytes 262144 | tf_op jit(solution)/shard_map/all_to_all | solution.py:213
  69.8 14.3 %all_to_all.22.x_ref = f32[16,8,128]{2,1,0:T(8,128)S(1)} all-to-all(f32[16,8,128]{2,1,0:T(8,128)S(1)} %sum_plane.1), channel_id=1, replica_groups=mesh['xh'=2,'y'=4,'c'=2,'z'=16,'xl'=2] {'z'}, dimensions={0} | all-to-all | bytes 131072 | tf_op jit(solution)/shard_map/all_to_all | solution.py:215
  84.0 12.8 %all_to_all.23.x_ref = f32[32,8,128]{2,1,0:T(8,128)S(1)} all-to-all(f32[32,8,128]{2,1,0:T(8,128)S(1)} %sum_z.1), channel_id=1, replica_groups=mesh['xh'=2,'y'=4,'c'=2,'z'=16,'xl'=2] {'xh','xl','y','c'}, dimensions={0} | all-to-all | bytes 262144 | tf_op jit(solution)/shard_map/all_to_all | solution.py:217
  96.8 0.7 unpack.1
  (2 shorter events, 0.1 us)
Async XLA Ops:
  1.7 10.7 %collective-permute-start.1 = (bf16[1,8192]{1,0:T(2,128)(2,1)S(1)}, bf16[1,8192]{1,0:T(2,128)(2,1)S(1)}, u32[]{:S(2)}, u32[]{:S(2)}) collective-permute-start(bf16[1,8192]{1,0:T(2,128)(2,1)S(1)} %get-tuple-element.14), channel_id=1, source_target_pairs={{32,0},{64,32},{96,64},{128,96},{160,128},{192,160},{224,192},{256... | collective-permute-start | bytes 49160 | tf_op jit(solution)/shard_map/ppermute | solution.py:190
  10.5 3.1 %collective-permute-start = (bf16[1,8192]{1,0:T(2,128)(2,1)S(1)}, bf16[1,8192]{1,0:T(2,128)(2,1)S(1)}, u32[]{:S(2)}, u32[]{:S(2)}) collective-permute-start(bf16[1,8192]{1,0:T(2,128)(2,1)S(1)} %get-tuple-element.15), channel_id=1, source_target_pairs={{0,32},{32,64},{64,96},{96,128},{128,160},{160,192},{192,224},{224... | collective-permute-start | bytes 49160 | tf_op jit(solution)/shard_map/ppermute | solution.py:189
  13.6 1.0 copy-start
  14.9 37.0 %copy-start.1 = (bf16[64,8,128]{2,1,0:T(8,128)(2,1)S(1)}, bf16[64,8,128]{2,1,0:T(8,128)(2,1)}, u32[]{:S(2)}) copy-start(bf16[64,8,128]{2,1,0:T(8,128)(2,1)} %cot_ref.1) | copy-start | bytes 393220
  14.9 36.9 %copy-start.2 = (bf16[64,32,3,3]{0,1,3,2:T(8,128)(2,1)S(1)}, bf16[64,32,3,3]{0,1,3,2:T(8,128)(2,1)}, u32[]{:S(2)}) copy-start(bf16[64,32,3,3]{0,1,3,2:T(8,128)(2,1)} %param.7) | copy-start | bytes 110596
  14.9 36.9 %copy-start.3 = (s32[16,256]{1,0:T(8,128)S(1)}, s32[16,256]{1,0:T(8,128)}, u32[]{:S(2)}) copy-start(s32[16,256]{1,0:T(8,128)} %mask_ref.1) | copy-start | bytes 49156
  51.8 0.7 copy-start.4
  51.8 0.7 copy-start.5

commit v2 on v1

v2 whole, which is shorter than its diff:
```python
import functools
import math

import jax
import jax.numpy as jnp
from jax import lax
from jax.experimental import pallas as pl
from jax.experimental.pallas import tpu as pltpu
from jax.sharding import Mesh
from jax.sharding import PartitionSpec as P

AXES = ("xh", "y", "c", "z", "xl")
LAT = ("xh", "y", "c")
LON = ("z", "xl")
PLANE = ("xh", "xl", "y", "c")
F32 = jnp.float32
BF16 = jnp.bfloat16
ROWS = 16
COLS = 256
LANES = 128
PIECE = 40
VMEM = pl.BlockSpec(memory_space=pltpu.VMEM)
ANY = pl.BlockSpec(memory_space=pl.ANY)
HBM = pl.BlockSpec(memory_space=pltpu.HBM)
SMEM = pl.BlockSpec(memory_space=pltpu.SMEM)


def iota(shape, dim):
    return lax.broadcasted_iota(jnp.int32, shape, dim)


def edge_lanes(tiles, tile, half):
    if half == 0:
        return 0, 64 + (tile - 1) % tiles
    return LANES - 1, (tile + 1) % tiles


def pack_kernel(tiles, core_ref, x_ref, outer_ref, inner_ref, edges_ref, out_ref):
    first = core_ref[0] == 0
    rows8 = iota((8, LANES), 0)
    lanes = iota((8, LANES), 1)
    beside = jnp.zeros((8, LANES), F32)
    tails = []
    for tile in range(tiles):
        for half in range(2):
            k = 2 * tile + half
            at = pl.ds(k * LANES, LANES)
            out_ref[tile, half * ROWS : (half + 1) * ROWS, :] = x_ref[:, at]
            outer = outer_ref[:, at].astype(F32)
            top = jnp.where(first, outer, inner_ref[k : k + 1, :])
            bottom = jnp.where(first, inner_ref[2 * tiles + k : 2 * tiles + k + 1, :], outer)
            tails.append((top, bottom))
            halo = jnp.where(rows8 == 0, top, jnp.where(rows8 == 1, bottom, 0.0))
            source, target = edge_lanes(tiles, tile, half)
            beside = jnp.where(lanes == target, pltpu.roll(halo, (target - source) % LANES, 1), beside)
    square = jnp.concatenate([edges_ref[...], beside, jnp.zeros((LANES - ROWS - 8, LANES), F32)], axis=0).T
    columns = square[:tiles] + pltpu.roll(square[64 : 64 + tiles], 64, 1)
    for tile in range(tiles):
        (top0, bottom0), (top1, bottom1) = tails[2 * tile : 2 * tile + 2]
        tail = jnp.where(rows8 == 0, top0, 0.0)
        tail = jnp.where(rows8 == 1, top1, tail)
        tail = jnp.where(rows8 == 2, bottom0, tail)
        tail = jnp.where(rows8 == 3, bottom1, tail)
        tail = jnp.where(rows8 == 4, columns[tile : tile + 1], tail)
        out_ref[tile, 2 * ROWS : PIECE, :] = tail.astype(BF16)


def column_of(row, count):
    return jnp.sum(jnp.where(iota((count, count), 0) == iota((count, count), 1), row, 0.0), axis=1, keepdims=True)


def edges_of(tiles, first, x_ref, outer_ref, inner_ref, edges_ref):
    lanes = iota((ROWS, LANES), 1)
    edges = jnp.zeros((ROWS, LANES), F32)
    for k in range(2 * tiles):
        at = pl.ds(k * LANES, LANES)
        block = x_ref[:, at].astype(F32)
        top, bottom = block[0:1], block[ROWS - 1 : ROWS]
        outer_ref[:, at] = jnp.where(first, top, bottom).astype(BF16)
        inner_ref[k : k + 1, :] = jnp.where(first, bottom, top)
        source, target = edge_lanes(tiles, k // 2, k % 2)
        edges = jnp.where(lanes == target, pltpu.roll(block, (target - source) % LANES, 1), edges)
    edges_ref[...] = edges


def first_kernel(
    tiles,
    factor,
    core_ref,
    x_in,
    w_in,
    bias_in,
    land_in,
    mask_in,
    cot_in,
    x_ref,
    outer_ref,
    inner_ref,
    edges_ref,
    w_out,
    bias_out,
    land_out,
    mask_out,
    wide_out,
    w_ref,
    bias_ref,
    land_ref,
    mask_ref,
    cot_ref,
    wide0,
    wide1,
    sems,
):
    pairs = [(x_in, x_ref), (cot_in, cot_ref), (w_in, w_ref), (bias_in, bias_ref), (land_in, land_ref), (mask_in, mask_ref)]
    copies = [pltpu.make_async_copy(source, target, sems.at[k]) for k, (source, target) in enumerate(pairs)]
    for copy in copies:
        copy.start()
    copies[0].wait()
    edges_of(tiles, core_ref[0] == 0, x_ref, outer_ref, inner_ref, edges_ref)
    for copy in copies[1:]:
        copy.wait()
    taps, channels = w_ref.shape
    pool_rows = ROWS // 2
    weight = w_ref[...].astype(F32).T
    zero = jnp.zeros((channels, taps // 3), F32)
    upper = jnp.concatenate([weight, zero], axis=1)
    lower = jnp.concatenate([zero, weight], axis=1)
    w_out[...] = jnp.concatenate([upper, lower], axis=0).astype(BF16)
    bias_out[...] = jnp.broadcast_to(column_of(bias_ref[...], channels), bias_out.shape)
    land_out[...] = jnp.broadcast_to(column_of(land_ref[...], channels), land_out.shape)
    mask_out[...] = mask_ref[...].astype(F32)
    spread = (iota((LANES, COLS), 1) // 2 == iota((LANES, COLS), 0)).astype(F32).astype(BF16)
    wide = jnp.dot(cot_ref[...].reshape(channels * pool_rows, LANES), spread, preferred_element_type=F32) * factor
    wide0[...] = wide[:, :LANES]
    wide1[...] = wide[:, LANES:]
    for p in range(pool_rows):
        here = pl.ds(p, channels, stride=pool_rows)
        wide_out[p] = jnp.concatenate([wide0[here, :], wide1[here, :]], axis=1)


def conv_kernel(r_ref, w_ref, bias_ref, land_ref, mask_ref, wide_ref, pooled_ref, sums_ref, flat_ref, patch_ref, low_ref, act0, act1, pooled_vmem, sem):
    fields = r_ref.shape[0]
    channels = bias_ref.shape[0]
    taps = 9 * fields
    pool_rows = ROWS // 2
    for c in range(fields):
        flat_ref[c * PIECE : (c + 1) * PIECE, :] = r_ref[c].astype(F32)

    def take(k):
        return flat_ref[pl.ds(k, fields, stride=PIECE), :]

    columns = take(36)
    first_lane = iota((fields, LANES), 1) == 0
    last_lane = iota((fields, LANES), 1) == LANES - 1
    for r in range(ROWS + 2):
        if r == 0:
            k0, k1, lane = 32, 33, 16
        elif r == ROWS + 1:
            k0, k1, lane = 34, 35, 17
        else:
            k0, k1, lane = r - 1, ROWS + r - 1, r - 1
        a, b = take(k0), take(k1)
        up_a, up_b = pltpu.roll(a, 1, 1), pltpu.roll(b, 1, 1)
        down_a, down_b = pltpu.roll(a, LANES - 1, 1), pltpu.roll(b, LANES - 1, 1)
        patch_ref[r, 0:fields, :LANES] = jnp.where(first_lane, columns[:, lane : lane + 1], up_a).astype(BF16)
        patch_ref[r, 0:fields, LANES:] = jnp.where(first_lane, up_a, up_b).astype(BF16)
        patch_ref[r, fields : 2 * fields, :LANES] = a.astype(BF16)
        patch_ref[r, fields : 2 * fields, LANES:] = b.astype(BF16)
        patch_ref[r, 2 * fields :, :LANES] = jnp.where(last_lane, down_b, down_a).astype(BF16)
        patch_ref[r, 2 * fields :, LANES:] = jnp.where(last_lane, columns[:, 64 + lane : 65 + lane], down_b).astype(BF16)

    root = math.sqrt(2.0 / math.pi)
    weight = w_ref[...]
    grad_b = jnp.zeros((channels, COLS), F32)
    grad_l = jnp.zeros((channels, COLS), F32)
    for p in range(pool_rows):
        grad_act = wide_ref[p]
        patch = patch_ref[2 * p : 2 * p + 4].reshape(4 * taps // 3, COLS)
        both = jnp.dot(weight, patch, preferred_element_type=F32)
        act = None
        for k in range(2):
            mask = mask_ref[2 * p + k : 2 * p + k + 1, :]
            v = both[k * channels : (k + 1) * channels] + (bias_ref[...] + land_ref[...] * mask)
            square = v * v
            t = jnp.tanh(v * (root + (root * 0.044715) * square))
            half = 0.5 + 0.5 * t
            gelu = v * half
            slope = half + gelu * (1.0 - t) * (root + (3.0 * root * 0.044715) * square)
            grad_pre = grad_act * slope
            low_ref[p, k * channels : (k + 1) * channels, :] = grad_pre.astype(BF16)
            grad_b += grad_pre
            grad_l += grad_pre * mask
            act = gelu if act is None else act + gelu
        here = pl.ds(p, channels, stride=pool_rows)
        act0[here, :] = act[:, :LANES]
        act1[here, :] = act[:, LANES:]

    pair = (iota((COLS, LANES), 0) // 2 == iota((COLS, LANES), 1)).astype(F32).astype(BF16)
    total = jnp.concatenate([act0[...], act1[...]], axis=1)
    high = total.astype(BF16)
    low = (total - high.astype(F32)).astype(BF16)
    pooled = jnp.dot(high, pair, preferred_element_type=F32) + jnp.dot(low, pair, preferred_element_type=F32)
    pooled_vmem[...] = (pooled * 0.25).astype(BF16).reshape(pooled_vmem.shape)
    copy = pltpu.make_async_copy(pooled_vmem, pooled_ref, sem)
    copy.start()

    grad_w = jnp.zeros((4 * taps // 3, 2 * channels), F32)
    for p in range(pool_rows):
        patch = patch_ref[2 * p : 2 * p + 4].reshape(4 * taps // 3, COLS)
        grad_w += lax.dot_general(patch, low_ref[p], (((1,), (1,)), ((), ())), preferred_element_type=F32)

    ones = jnp.ones((8, COLS), F32)

    def across(grad):
        return lax.dot_general(
            ones, grad, (((1,), (1,)), ((), ())), precision=lax.Precision.HIGHEST, preferred_element_type=F32
        )

    half_taps = taps // 2
    used = half_taps // 8
    grad = grad_w[:taps, :channels] + grad_w[taps // 3 :, channels:]
    sums_ref[0:used] = jnp.concatenate([grad[:half_taps], grad[half_taps:]], axis=1).reshape(used, 8, LANES)
    sums_ref[used] = jnp.concatenate([across(grad_b), across(grad_l)], axis=1)
    sums_ref[used + 1 :] = jnp.zeros((sums_ref.shape[0] - used - 1, 8, LANES), F32)
    copy.wait()


def sum_kernel(x_ref, out_ref):
    out_ref[...] = jnp.broadcast_to(jnp.sum(x_ref[...], axis=0, keepdims=True), out_ref.shape)


def unpack_kernel(x_ref, weight_ref, bias_ref, land_ref):
    half_taps = weight_ref.shape[0] // 2
    channels = weight_ref.shape[1]
    used = half_taps // 8
    both = x_ref[0:used].reshape(half_taps, LANES)
    weight_ref[0:half_taps, :] = both[:, :channels]
    weight_ref[half_taps:, :] = both[:, channels:]
    bias_ref[...] = x_ref[used, 0:1, :channels]
    land_ref[...] = x_ref[used, 0:1, channels:]


def call(kernel, name, outs, *args, scratch=(), scalars=0, places=None, out_places=None, limit=32):
    shapes = [jax.ShapeDtypeStruct(*o) for o in outs]
    single = len(shapes) == 1
    return pl.pallas_call(
        kernel,
        name=name,
        out_shape=shapes[0] if single else shapes,
        in_specs=places or [SMEM] * scalars + [VMEM] * (len(args) - scalars),
        out_specs=out_places or (VMEM if single else [VMEM] * len(shapes)),
        scratch_shapes=list(scratch),
        compiler_params=pltpu.CompilerParams(vmem_limit_bytes=limit * 1024 * 1024),
    )(*args)


def local(fields, weight, bias, land_bias, land_mask, cotangent):
    channels, in_fields = weight.shape[:2]
    taps = 9 * in_fields
    tiles = lax.axis_size(LON)
    rows_count = lax.axis_size(LAT)
    members = lax.axis_size(PLANE)
    pool_rows = ROWS // 2
    columns = fields.shape[2]
    core = lax.axis_index("c").reshape(1)
    factor = 0.25 / math.sqrt(float(cotangent.shape[1] * rows_count * cotangent.shape[2] * tiles))
    field, outer, inner, edges, *prepared = call(
        functools.partial(first_kernel, tiles, factor),
        "first",
        [
            ((ROWS, columns), BF16),
            ((1, columns), BF16),
            ((columns // LANES, LANES), F32),
            ((ROWS, LANES), F32),
            ((2 * channels, 4 * taps // 3), BF16),
            ((channels, COLS), F32),
            ((channels, COLS), F32),
            ((ROWS, COLS), F32),
            ((pool_rows, channels, COLS), F32),
        ],
        core,
        *(
            pltpu.with_memory_space_constraint(given, pltpu.HBM)
            for given in (
                fields[0],
                weight.transpose(2, 3, 1, 0).reshape(taps, channels),
                bias.reshape(1, channels),
                land_bias.reshape(1, channels),
                land_mask,
                cotangent,
            )
        ),
        scratch=[
            pltpu.VMEM((taps, channels), BF16),
            pltpu.VMEM((1, channels), F32),
            pltpu.VMEM((1, channels), F32),
            pltpu.VMEM(land_mask.shape, jnp.int32),
            pltpu.VMEM(cotangent.shape, BF16),
            pltpu.VMEM((channels * pool_rows, LANES), F32),
            pltpu.VMEM((channels * pool_rows, LANES), F32),
            pltpu.SemaphoreType.DMA((6,)),
        ],
        places=[SMEM] + [HBM] * 6,
        limit=32,
    )
    swap = [pair for i in range(1, rows_count - 1, 2) for pair in ((i, i + 1), (i + 1, i))]
    outer = lax.ppermute(outer, LAT, swap)
    inner = lax.all_gather(inner, "c", axis=0, tiled=True)
    pieces = call(
        functools.partial(pack_kernel, tiles),
        "pack",
        [((tiles, PIECE, LANES), BF16)],
        core,
        field,
        outer,
        inner,
        edges,
        scalars=1,
    )
    pieces = lax.all_to_all(pieces, LON, 0, 0, tiled=True)
    pooled, sums = call(
        conv_kernel,
        "conv",
        [(cotangent.shape, BF16), ((members, 8, LANES), F32)],
        pieces,
        *prepared,
        scratch=[
            pltpu.VMEM((in_fields * PIECE, LANES), F32),
            pltpu.VMEM((ROWS + 2, 3 * in_fields, COLS), BF16),
            pltpu.VMEM((pool_rows, 2 * channels, COLS), BF16),
            pltpu.VMEM((channels * pool_rows, LANES), F32),
            pltpu.VMEM((channels * pool_rows, LANES), F32),
            pltpu.VMEM(cotangent.shape, BF16),
            pltpu.SemaphoreType.DMA,
        ],
        out_places=[ANY, VMEM],
    )
    sums = lax.all_to_all(sums, PLANE, 0, 0, tiled=True)
    sums = call(sum_kernel, "sum_plane", [((lax.axis_size("z"), 8, LANES), F32)], sums)
    sums = lax.all_to_all(sums, "z", 0, 0, tiled=True)
    sums = call(sum_kernel, "sum_z", [((members, 8, LANES), F32)], sums)
    sums = lax.all_to_all(sums, PLANE, 0, 0, tiled=True)
    grad_weight, grad_bias, grad_land = call(
        unpack_kernel,
        "unpack",
        [((taps, channels), F32), ((1, channels), F32), ((1, channels), F32)],
        sums,
    )
    grad_weight = grad_weight.reshape(3, 3, in_fields, channels).transpose(3, 2, 0, 1)
    return pooled, grad_weight, grad_bias.reshape(channels), grad_land.reshape(channels)


def solution(mesh):
    physical = Mesh(mesh.devices.reshape(2, 4, 2, 16, 2), AXES)
    placed = (P(LON, LAT, None), P(), P(), P(), P(LAT, LON), P(None, LAT, LON))
    return jax.shard_map(
        local,
        mesh=physical,
        in_specs=placed,
        out_specs=(P(None, LAT, LON), P(), P(), P()),
        check_vma=False,
    )
```

time: 97.9 us -> 94.9 us (0.969)
  starting transfers between devices: 10.7 us -> 4.59 us
  blocking collectives: 78.6 us -> 84.5 us
  local copies, waits for them, and re-layouts: 2.65 us -> 0 us
  waiting for transfers between devices: 1.17 us -> 0.01 us
  Pallas kernels: 3.69 us -> 4.82 us
    ppermute x2 -> x1, starting transfers between devices: 10.7 us -> 4.59 us  [local(): outer = lax.ppermute(outer, LAT, swap)]
    all_gather x0 -> x1, blocking collectives: none -> 4.45 us  [local(): inner = lax.all_gather(inner, 'c', axis=0, tiled=True)]
    unnamed x12 -> x0, local copies, waits for them, and re-layouts: 1.62 us -> none
    ppermute x2 -> x1, waiting for transfers between devices: 1.17 us -> 0.01 us  [local(): outer = lax.ppermute(outer, LAT, swap)]
    pallas_call x5 -> x6, Pallas kernels: 3.69 us -> 4.82 us  [call(): pl.pallas_call(kernel, name=name, out_shape=shapes[0] if single else shap...]
    slice x1 -> x0, local copies, waits for them, and re-layouts: 1.03 us -> none  [local(): bottom = lax.ppermute(field[:1], LAT, down)]
    all_to_all x2, blocking collectives: 27.5 us -> 28.5 us  [local(): sums = lax.all_to_all(sums, PLANE, 0, 0, tiled=True)]
  transfers between devices with their start and end apart: 2 -> 1, of which waited for: 1 -> 0; matrix products, arithmetic and copies ran while one was open for 0% -> 0% of each run, Pallas kernels for 0% -> 0%
where the time goes in v2:
time: 94.9 us; the launch traced here: 94.6 us
  blocking collectives  84.5 us (89%)
  Pallas kernels  4.82 us (5%)
  starting transfers between devices  4.59 us (5%)
    all_to_all x1, blocking collectives, local(): pieces = lax.all_to_all(pieces, LON, 0, 0, tiled=True)  37.3 us
    all_to_all x2, blocking collectives, local(): sums = lax.all_to_all(sums, PLANE, 0, 0, tiled=True)  28.5 us
    all_to_all x1, blocking collectives, local(): sums = lax.all_to_all(sums, 'z', 0, 0, tiled=True)  14.3 us
    pallas_call x6, Pallas kernels, call(): pl.pallas_call(kernel, name=name, out_shape=shapes[0] if single else shap...  4.82 us
    ppermute x1, starting transfers between devices, local(): outer = lax.ppermute(outer, LAT, swap)  4.59 us
    all_gather x1, blocking collectives, local(): inner = lax.all_gather(inner, 'c', axis=0, tiled=True)  4.45 us
  transfers between devices with their start and end apart: 1, of which 0 were waited for; matrix products, arithmetic and copies ran while one was open for 0% of the time, Pallas kernels for 0%

profile of v2, /device:TPU:1, one launch (start us, length us, event | category | flops | bytes accessed | tf_op | source)
XLA Modules:
  0.0 94.6 jit_solution(16800529091909953042)
XLA Ops:
  0.6 1.5 %first.1 = (bf16[16,8192]{1,0:T(8,128)(2,1)S(1)}, bf16[1,8192]{1,0:T(2,128)(2,1)S(1)}, f32[64,128]{1,0:T(8,128)S(1)}, f32[16,128]{1,0:T(8,128)S(1)}, bf16[128,38...) custom-call(s32[1]{0:T(128)} %bitcast.core_ref, ...), custom_call_target="tpu_custom_call" | custom-call | tf_op jit(solution)/shard_map/first/pallas_call | solution.py:246
  2.1 4.6 %collective-permute-start = (bf16[1,8192]{1,0:T(2,128)(2,1)S(1)}, bf16[1,8192]{1,0:T(2,128)(2,1)S(1)}, u32[]{:S(2)}, u32[]{:S(2)}) collective-permute-start(bf16[1,8192]{1,0:T(2,128)(2,1)S(1)} %get-tuple-element.19), channel_id=1, source_target_pairs={{32,64},{64,32},{96,128},{128,96},{160,192},{192,160},{224,256},{2... | collective-permute-start | bytes 49160 | tf_op jit(solution)/shard_map/ppermute | solution.py:307
  6.7 4.5 %all_gather.3.inner_ref = f32[128,128]{1,0:T(8,128)S(1)} all-gather(f32[64,128]{1,0:T(8,128)S(1)} %get-tuple-element.20), channel_id=1, replica_groups=mesh['xh'=2,'y'=4,'c'=2,'z'=16,'xl'=2] {'c'}, dimensions={0}, use_global_device_ids=true | all-gather | bytes 98304 | tf_op jit(solution)/shard_map/all_gather | solution.py:308
  11.2 0.0 collective-permute-done.outer_ref
  11.2 0.3 pack.1
  11.5 37.3 %all_to_all.20.r_ref = bf16[32,40,128]{2,1,0:T(8,128)(2,1)S(1)} all-to-all(bf16[32,40,128]{2,1,0:T(8,128)(2,1)S(1)} %pack.1), channel_id=1, replica_groups=mesh['xh'=2,'y'=4,'c'=2,'z'=16,'xl'=2] {'z','xl'}, dimensions={0} | all-to-all | bytes 655360 | tf_op jit(solution)/shard_map/all_to_all | solution.py:320
  48.8 2.2 %conv.1 = (bf16[64,8,128]{2,1,0:T(8,128)(2,1)}, f32[32,8,128]{2,1,0:T(8,128)S(1)}) custom-call(bf16[32,40,128]{2,1,0:T(8,128)(2,1)S(1)} %all_to_all.20.r_ref, bf16[128,384]{1,0:T(8,128)(2,1)S(1)} %get-tuple-element.22.w_ref, f32[64,256]{1,0:T(8,128)S(1)} %get-tuple-element.23.bias_ref, f32[64,256]{1,0:T(8,128)S(1)} %get-tuple-element.24.land_ref, ...), custom_call_target="tpu_custom_call" | custom-call | tf_op jit(solution)/shard_map/conv/pallas_call | solution.py:246
  51.0 15.8 %all_to_all.21.x_ref = f32[32,8,128]{2,1,0:T(8,128)S(1)} all-to-all(f32[32,8,128]{2,1,0:T(8,128)S(1)} %get-tuple-element.28), channel_id=1, replica_groups=mesh['xh'=2,'y'=4,'c'=2,'z'=16,'xl'=2] {'xh','xl','y','c'}, dimensions={0} | all-to-all | bytes 262144 | tf_op jit(solution)/shard_map/all_to_all | solution.py:338
  66.9 14.3 %all_to_all.22.x_ref = f32[16,8,128]{2,1,0:T(8,128)S(1)} all-to-all(f32[16,8,128]{2,1,0:T(8,128)S(1)} %sum_plane.1), channel_id=1, replica_groups=mesh['xh'=2,'y'=4,'c'=2,'z'=16,'xl'=2] {'z'}, dimensions={0} | all-to-all | bytes 131072 | tf_op jit(solution)/shard_map/all_to_all | solution.py:340
  81.2 12.6 %all_to_all.23.x_ref = f32[32,8,128]{2,1,0:T(8,128)S(1)} all-to-all(f32[32,8,128]{2,1,0:T(8,128)S(1)} %sum_z.1), channel_id=1, replica_groups=mesh['xh'=2,'y'=4,'c'=2,'z'=16,'xl'=2] {'xh','xl','y','c'}, dimensions={0} | all-to-all | bytes 262144 | tf_op jit(solution)/shard_map/all_to_all | solution.py:342
  93.8 0.7 unpack.1
  (2 shorter events, 0.1 us)
Async XLA Ops:
  2.1 9.1 %collective-permute-start = (bf16[1,8192]{1,0:T(2,128)(2,1)S(1)}, bf16[1,8192]{1,0:T(2,128)(2,1)S(1)}, u32[]{:S(2)}, u32[]{:S(2)}) collective-permute-start(bf16[1,8192]{1,0:T(2,128)(2,1)S(1)} %get-tuple-element.19), channel_id=1, source_target_pairs={{32,64},{64,32},{96,128},{128,96},{160,192},{192,160},{224,256},{2... | collective-permute-start | bytes 49160 | tf_op jit(solution)/shard_map/ppermute | solution.py:307

commit v3 on v2

--- a/solution.py
+++ b/solution.py
@@ -84,32 +84,7 @@
 
 
 def first_kernel(
-    tiles,
-    factor,
-    core_ref,
-    x_in,
-    w_in,
-    bias_in,
-    land_in,
-    mask_in,
-    cot_in,
-    x_ref,
-    outer_ref,
-    inner_ref,
-    edges_ref,
-    w_out,
-    bias_out,
-    land_out,
-    mask_out,
-    wide_out,
-    w_ref,
-    bias_ref,
-    land_ref,
-    mask_ref,
-    cot_ref,
-    wide0,
-    wide1,
-    sems,
+    tiles, core_ref, x_in, w_in, bias_in, land_in, mask_in, cot_in, x_ref, w_ref, bias_ref, land_ref, mask_ref, cot_ref, outer_ref, inner_ref, edges_ref, sems
 ):
     pairs = [(x_in, x_ref), (cot_in, cot_ref), (w_in, w_ref), (bias_in, bias_ref), (land_in, land_ref), (mask_in, mask_ref)]
     copies = [pltpu.make_async_copy(source, target, sems.at[k]) for k, (source, target) in enumerate(pairs)]
@@ -119,6 +94,10 @@
     edges_of(tiles, core_ref[0] == 0, x_ref, outer_ref, inner_ref, edges_ref)
     for copy in copies[1:]:
         copy.wait()
+
+
+def prepare_kernel(factor, w_ref, bias_ref, land_ref, mask_ref, cot_ref, after_ref, w_out, bias_out, land_out, mask_out, wide_out, wide0, wide1):
+    del after_ref
     taps, channels = w_ref.shape
     pool_rows = ROWS // 2
     weight = w_ref[...].astype(F32).T
@@ -138,7 +117,7 @@
         wide_out[p] = jnp.concatenate([wide0[here, :], wide1[here, :]], axis=1)
 
 
-def conv_kernel(r_ref, w_ref, bias_ref, land_ref, mask_ref, wide_ref, pooled_ref, sums_ref, flat_ref, patch_ref, low_ref, act0, act1, pooled_vmem, sem):
+def conv_kernel(r_ref, w_ref, bias_ref, land_ref, mask_ref, wide_ref, pooled_ref, sums_ref, flat_ref, patch_ref, low_ref, act0, act1):
     fields = r_ref.shape[0]
     channels = bias_ref.shape[0]
     taps = 9 * fields
@@ -195,53 +174,54 @@
         act0[here, :] = act[:, :LANES]
         act1[here, :] = act[:, LANES:]
 
-    pair = (iota((COLS, LANES), 0) // 2 == iota((COLS, LANES), 1)).astype(F32).astype(BF16)
-    total = jnp.concatenate([act0[...], act1[...]], axis=1)
-    high = total.astype(BF16)
-    low = (total - high.astype(F32)).astype(BF16)
-    pooled = jnp.dot(high, pair, preferred_element_type=F32) + jnp.dot(low, pair, preferred_element_type=F32)
-    pooled_vmem[...] = (pooled * 0.25).astype(BF16).reshape(pooled_vmem.shape)
-    copy = pltpu.make_async_copy(pooled_vmem, pooled_ref, sem)
-    copy.start()
-
     grad_w = jnp.zeros((4 * taps // 3, 2 * channels), F32)
     for p in range(pool_rows):
         patch = patch_ref[2 * p : 2 * p + 4].reshape(4 * taps // 3, COLS)
         grad_w += lax.dot_general(patch, low_ref[p], (((1,), (1,)), ((), ())), preferred_element_type=F32)
 
-    ones = jnp.ones((8, COLS), F32)
-
     def across(grad):
-        return lax.dot_general(
-            ones, grad, (((1,), (1,)), ((), ())), precision=lax.Precision.HIGHEST, preferred_element_type=F32
-        )
+        column = jnp.sum(grad, axis=1, keepdims=True)
+        eye = iota((channels, channels), 0) == iota((channels, channels), 1)
+        return jnp.sum(jnp.where(eye, column, 0.0), axis=0, keepdims=True)
 
     half_taps = taps // 2
     used = half_taps // 8
     grad = grad_w[:taps, :channels] + grad_w[taps // 3 :, channels:]
     sums_ref[0:used] = jnp.concatenate([grad[:half_taps], grad[half_taps:]], axis=1).reshape(used, 8, LANES)
-    sums_ref[used] = jnp.concatenate([across(grad_b), across(grad_l)], axis=1)
+    sums_ref[used] = jnp.broadcast_to(jnp.concatenate([across(grad_b), across(grad_l)], axis=1), (8, LANES))
     sums_ref[used + 1 :] = jnp.zeros((sums_ref.shape[0] - used - 1, 8, LANES), F32)
-    copy.wait()
+    pair = (iota((COLS, LANES), 0) == 2 * iota((COLS, LANES), 1)).astype(F32).astype(BF16)
+    halves = [((act[...] + pltpu.roll(act[...], LANES - 1, 1)) * 0.25).astype(BF16) for act in (act0, act1)]
+    pooled = jnp.dot(jnp.concatenate(halves, axis=1), pair, preferred_element_type=F32)
+    pooled_ref[...] = pooled.astype(BF16).reshape(pooled_ref.shape)
 
 
 def sum_kernel(x_ref, out_ref):
     out_ref[...] = jnp.broadcast_to(jnp.sum(x_ref[...], axis=0, keepdims=True), out_ref.shape)
 
 
-def unpack_kernel(x_ref, weight_ref, bias_ref, land_ref):
-    half_taps = weight_ref.shape[0] // 2
-    channels = weight_ref.shape[1]
+def unpack_kernel(x_ref, pooled_ref, weight_out, bias_out, land_out, pooled_out, weight_ref, rows_ref, sems):
+    pooled_copy = pltpu.make_async_copy(pooled_ref, pooled_out, sems.at[3])
+    pooled_copy.start()
+    taps, channels = weight_ref.shape
+    half_taps = taps // 2
     used = half_taps // 8
+    rows_ref[0:1, :] = x_ref[used, 0:1, :channels]
+    rows_ref[8:9, :] = x_ref[used, 0:1, channels:]
     both = x_ref[0:used].reshape(half_taps, LANES)
     weight_ref[0:half_taps, :] = both[:, :channels]
     weight_ref[half_taps:, :] = both[:, channels:]
-    bias_ref[...] = x_ref[used, 0:1, :channels]
-    land_ref[...] = x_ref[used, 0:1, channels:]
+    pairs = ((weight_ref, weight_out), (rows_ref.at[0:1], bias_out), (rows_ref.at[8:9], land_out))
+    copies = [pltpu.make_async_copy(source, target, sems.at[k]) for k, (source, target) in enumerate(pairs)]
+    for copy in copies:
+        copy.start()
+    for copy in copies:
+        copy.wait()
+    pooled_copy.wait()
 
 
 def call(kernel, name, outs, *args, scratch=(), scalars=0, places=None, out_places=None, limit=32):
-    shapes = [jax.ShapeDtypeStruct(*o) for o in outs]
+    shapes = [o if isinstance(o, pl.MemoryRef) else jax.ShapeDtypeStruct(*o) for o in outs]
     single = len(shapes) == 1
     return pl.pallas_call(
         kernel,
@@ -264,54 +244,50 @@
     columns = fields.shape[2]
     core = lax.axis_index("c").reshape(1)
     factor = 0.25 / math.sqrt(float(cotangent.shape[1] * rows_count * cotangent.shape[2] * tiles))
-    field, outer, inner, edges, *prepared = call(
-        functools.partial(first_kernel, tiles, factor),
+    given = (
+        fields[0],
+        weight.transpose(2, 3, 1, 0).reshape(taps, channels),
+        bias.reshape(1, channels),
+        land_bias.reshape(1, channels),
+        land_mask,
+        cotangent,
+    )
+    *held, outer, inner, edges = call(
+        functools.partial(first_kernel, tiles),
         "first",
+        [(array.shape, array.dtype) for array in given]
+        + [((1, columns), BF16), ((columns // LANES, LANES), F32), ((ROWS, LANES), F32)],
+        core,
+        *(pltpu.with_memory_space_constraint(array, pltpu.HBM) for array in given),
+        scratch=[pltpu.SemaphoreType.DMA((6,))],
+        places=[SMEM] + [HBM] * 6,
+    )
+    swap = [pair for i in range(1, rows_count - 1, 2) for pair in ((i, i + 1), (i + 1, i))]
+    outer = lax.ppermute(outer, LAT, swap)
+    inner = lax.all_gather(inner, "c", axis=0, tiled=True)
+    after = inner
+    prepared = call(
+        functools.partial(prepare_kernel, factor),
+        "prepare",
         [
-            ((ROWS, columns), BF16),
-            ((1, columns), BF16),
-            ((columns // LANES, LANES), F32),
-            ((ROWS, LANES), F32),
             ((2 * channels, 4 * taps // 3), BF16),
             ((channels, COLS), F32),
             ((channels, COLS), F32),
             ((ROWS, COLS), F32),
             ((pool_rows, channels, COLS), F32),
         ],
-        core,
-        *(
-            pltpu.with_memory_space_constraint(given, pltpu.HBM)
-            for given in (
-                fields[0],
-                weight.transpose(2, 3, 1, 0).reshape(taps, channels),
-                bias.reshape(1, channels),
-                land_bias.reshape(1, channels),
-                land_mask,
-                cotangent,
-            )
-        ),
-        scratch=[
-            pltpu.VMEM((taps, channels), BF16),
-            pltpu.VMEM((1, channels), F32),
-            pltpu.VMEM((1, channels), F32),
-            pltpu.VMEM(land_mask.shape, jnp.int32),
-            pltpu.VMEM(cotangent.shape, BF16),
-            pltpu.VMEM((channels * pool_rows, LANES), F32),
-            pltpu.VMEM((channels * pool_rows, LANES), F32),
-            pltpu.SemaphoreType.DMA((6,)),
-        ],
-        places=[SMEM] + [HBM] * 6,
-        limit=32,
-    )
-    swap = [pair for i in range(1, rows_count - 1, 2) for pair in ((i, i + 1), (i + 1, i))]
-    outer = lax.ppermute(outer, LAT, swap)
-    inner = lax.all_gather(inner, "c", axis=0, tiled=True)
+        *held[1:],
+        after,
+        scratch=[pltpu.VMEM((channels * pool_rows, LANES), F32)] * 2,
+        places=[VMEM] * 5 + [ANY],
+    )
+    outer, inner, prepared = lax.optimization_barrier((outer, inner, prepared))
     pieces = call(
         functools.partial(pack_kernel, tiles),
         "pack",
         [((tiles, PIECE, LANES), BF16)],
         core,
-        field,
+        held[0],
         outer,
         inner,
         edges,
@@ -321,7 +297,7 @@
     pooled, sums = call(
         conv_kernel,
         "conv",
-        [(cotangent.shape, BF16), ((members, 8, LANES), F32)],
+        [pltpu.VMEM(cotangent.shape, BF16), ((members, 8, LANES), F32)],
         pieces,
         *prepared,
         scratch=[
@@ -330,21 +306,25 @@
             pltpu.VMEM((pool_rows, 2 * channels, COLS), BF16),
             pltpu.VMEM((channels * pool_rows, LANES), F32),
             pltpu.VMEM((channels * pool_rows, LANES), F32),
-            pltpu.VMEM(cotangent.shape, BF16),
-            pltpu.SemaphoreType.DMA,
         ],
-        out_places=[ANY, VMEM],
     )
     sums = lax.all_to_all(sums, PLANE, 0, 0, tiled=True)
     sums = call(sum_kernel, "sum_plane", [((lax.axis_size("z"), 8, LANES), F32)], sums)
     sums = lax.all_to_all(sums, "z", 0, 0, tiled=True)
     sums = call(sum_kernel, "sum_z", [((members, 8, LANES), F32)], sums)
     sums = lax.all_to_all(sums, PLANE, 0, 0, tiled=True)
-    grad_weight, grad_bias, grad_land = call(
+    grad_weight, grad_bias, grad_land, pooled = call(
         unpack_kernel,
         "unpack",
-        [((taps, channels), F32), ((1, channels), F32), ((1, channels), F32)],
+        [((taps, channels), F32), ((1, channels), F32), ((1, channels), F32), (cotangent.shape, BF16)],
         sums,
+        pooled,
+        scratch=[
+            pltpu.VMEM((taps, channels), F32),
+            pltpu.VMEM((16, channels), F32),
+            pltpu.SemaphoreType.DMA((4,)),
+        ],
+        out_places=[ANY] * 4,
     )
     grad_weight = grad_weight.reshape(3, 3, in_fields, channels).transpose(3, 2, 0, 1)
     return pooled, grad_weight, grad_bias.reshape(channels), grad_land.reshape(channels)

time: 94.9 us -> 94.4 us (level)
    pallas_call x6 -> x7, Pallas kernels: 4.82 us -> 4.51 us  [call(): pl.pallas_call(kernel, name=name, out_shape=shapes[0] if single else shap...]
where the time goes in v3:
time: 94.4 us; the launch traced here: 94.1 us
  blocking collectives  84.3 us (89%)
  starting transfers between devices  4.59 us (5%)
  Pallas kernels  4.51 us (5%)
    all_to_all x1, blocking collectives, local(): pieces = lax.all_to_all(pieces, LON, 0, 0, tiled=True)  37.1 us
    all_to_all x2, blocking collectives, local(): sums = lax.all_to_all(sums, PLANE, 0, 0, tiled=True)  28.5 us
    all_to_all x1, blocking collectives, local(): sums = lax.all_to_all(sums, 'z', 0, 0, tiled=True)  14.3 us
    ppermute x1, starting transfers between devices, local(): outer = lax.ppermute(outer, LAT, swap)  4.59 us
    pallas_call x7, Pallas kernels, call(): pl.pallas_call(kernel, name=name, out_shape=shapes[0] if single else shap...  4.51 us
    all_gather x1, blocking collectives, local(): inner = lax.all_gather(inner, 'c', axis=0, tiled=True)  4.45 us
  transfers between devices with their start and end apart: 1, of which 0 were waited for; matrix products, arithmetic and copies ran while one was open for 0% of the time, Pallas kernels for 0%

profile of v3, /device:TPU:1, one launch (start us, length us, event | category | flops | bytes accessed | tf_op | source)
XLA Modules:
  0.0 94.1 jit_solution(2598215493401050348)
XLA Ops:
  0.6 1.2 %first.1 = (bf16[16,8192]{1,0:T(8,128)(2,1)S(1)}, bf16[288,64]{1,0:T(8,128)(2,1)S(1)}, f32[1,64]{1,0:T(1,128)S(1)}, f32[1,64]{1,0:T(1,128)S(1)}, s32[16,256]{1,0...) custom-call(s32[1]{0:T(128)} %bitcast.core_ref, ...), custom_call_target="tpu_custom_call" | custom-call | tf_op jit(solution)/shard_map/first/pallas_call | solution.py:226
  1.8 4.6 %collective-permute-start = (bf16[1,8192]{1,0:T(2,128)(2,1)S(1)}, bf16[1,8192]{1,0:T(2,128)(2,1)S(1)}, u32[]{:S(2)}, u32[]{:S(2)}) collective-permute-start(bf16[1,8192]{1,0:T(2,128)(2,1)S(1)} %get-tuple-element.32), channel_id=1, source_target_pairs={{32,64},{64,32},{96,128},{128,96},{160,192},{192,160},{224,256},{2... | collective-permute-start | bytes 49160 | tf_op jit(solution)/shard_map/ppermute | solution.py:266
  6.4 4.5 %all_gather.3.after_ref.inner_ref = f32[128,128]{1,0:T(8,128)S(1)} all-gather(f32[64,128]{1,0:T(8,128)S(1)} %get-tuple-element.33), channel_id=1, replica_groups=mesh['xh'=2,'y'=4,'c'=2,'z'=16,'xl'=2] {'c'}, dimensions={0}, use_global_device_ids=true | all-gather | bytes 98304 | tf_op jit(solution)/shard_map/all_gather | solution.py:267
  10.9 0.3 prepare.1
  11.2 0.0 collective-permute-done.outer_ref
  11.2 0.3 pack.1
  11.5 37.1 %all_to_all.20.r_ref = bf16[32,40,128]{2,1,0:T(8,128)(2,1)S(1)} all-to-all(bf16[32,40,128]{2,1,0:T(8,128)(2,1)S(1)} %pack.1), channel_id=1, replica_groups=mesh['xh'=2,'y'=4,'c'=2,'z'=16,'xl'=2] {'z','xl'}, dimensions={0} | all-to-all | bytes 655360 | tf_op jit(solution)/shard_map/all_to_all | solution.py:296
  48.6 1.9 %conv.1 = (bf16[64,8,128]{2,1,0:T(8,128)(2,1)S(1)}, f32[32,8,128]{2,1,0:T(8,128)S(1)}) custom-call(bf16[32,40,128]{2,1,0:T(8,128)(2,1)S(1)} %all_to_all.20.r_ref, bf16[128,384]{1,0:T(8,128)(2,1)S(1)} %get-tuple-element.47.w_ref, f32[64,256]{1,0:T(8,128)S(1)} %get-tuple-element.48.bias_ref, f32[64,256]{1,0:T(8,128)S(1)} %get-tuple-element.49.land_ref, ...), custom_call_target="tpu_custom_call" | custom-call | tf_op jit(solution)/shard_map/conv/pallas_call | solution.py:226
  50.5 15.9 %all_to_all.21.x_ref = f32[32,8,128]{2,1,0:T(8,128)S(1)} all-to-all(f32[32,8,128]{2,1,0:T(8,128)S(1)} %get-tuple-element.52), channel_id=1, replica_groups=mesh['xh'=2,'y'=4,'c'=2,'z'=16,'xl'=2] {'xh','xl','y','c'}, dimensions={0} | all-to-all | bytes 262144 | tf_op jit(solution)/shard_map/all_to_all | solution.py:311
  66.4 14.3 %all_to_all.22.x_ref = f32[16,8,128]{2,1,0:T(8,128)S(1)} all-to-all(f32[16,8,128]{2,1,0:T(8,128)S(1)} %sum_plane.1), channel_id=1, replica_groups=mesh['xh'=2,'y'=4,'c'=2,'z'=16,'xl'=2] {'z'}, dimensions={0} | all-to-all | bytes 131072 | tf_op jit(solution)/shard_map/all_to_all | solution.py:313
  80.7 12.6 %all_to_all.23.x_ref = f32[32,8,128]{2,1,0:T(8,128)S(1)} all-to-all(f32[32,8,128]{2,1,0:T(8,128)S(1)} %sum_z.1), channel_id=1, replica_groups=mesh['xh'=2,'y'=4,'c'=2,'z'=16,'xl'=2] {'xh','xl','y','c'}, dimensions={0} | all-to-all | bytes 262144 | tf_op jit(solution)/shard_map/all_to_all | solution.py:315
  93.3 0.8 unpack.1
  (2 shorter events, 0.1 us)
Async XLA Ops:
  1.8 9.4 %collective-permute-start = (bf16[1,8192]{1,0:T(2,128)(2,1)S(1)}, bf16[1,8192]{1,0:T(2,128)(2,1)S(1)}, u32[]{:S(2)}, u32[]{:S(2)}) collective-permute-start(bf16[1,8192]{1,0:T(2,128)(2,1)S(1)} %get-tuple-element.32), channel_id=1, source_target_pairs={{32,64},{64,32},{96,128},{128,96},{160,192},{192,160},{224,256},{2... | collective-permute-start | bytes 49160 | tf_op jit(solution)/shard_map/ppermute | solution.py:266

commit v4 on v3

--- a/solution.py
+++ b/solution.py
@@ -29,6 +29,14 @@
     return lax.broadcasted_iota(jnp.int32, shape, dim)
 
 
+def turned(index, count):
+    return (index + count // 2) % count
+
+
+def from_far(count, start):
+    return [[(i + start) % count for i in range(count)]]
+
+
 def edge_lanes(tiles, tile, half):
     if half == 0:
         return 0, 64 + (tile - 1) % tiles
@@ -45,7 +53,7 @@
         for half in range(2):
             k = 2 * tile + half
             at = pl.ds(k * LANES, LANES)
-            out_ref[tile, half * ROWS : (half + 1) * ROWS, :] = x_ref[:, at]
+            out_ref[turned(tile, tiles), half * ROWS : (half + 1) * ROWS, :] = x_ref[:, at]
             outer = outer_ref[:, at].astype(F32)
             top = jnp.where(first, outer, inner_ref[k : k + 1, :])
             bottom = jnp.where(first, inner_ref[2 * tiles + k : 2 * tiles + k + 1, :], outer)
@@ -62,7 +70,7 @@
         tail = jnp.where(rows8 == 2, bottom0, tail)
         tail = jnp.where(rows8 == 3, bottom1, tail)
         tail = jnp.where(rows8 == 4, columns[tile : tile + 1], tail)
-        out_ref[tile, 2 * ROWS : PIECE, :] = tail.astype(BF16)
+        out_ref[turned(tile, tiles), 2 * ROWS : PIECE, :] = tail.astype(BF16)
 
 
 def column_of(row, count):
@@ -123,7 +131,7 @@
     taps = 9 * fields
     pool_rows = ROWS // 2
     for c in range(fields):
-        flat_ref[c * PIECE : (c + 1) * PIECE, :] = r_ref[c].astype(F32)
+        flat_ref[c * PIECE : (c + 1) * PIECE, :] = r_ref[turned(c, fields)].astype(F32)
 
     def take(k):
         return flat_ref[pl.ds(k, fields, stride=PIECE), :]
@@ -293,7 +301,7 @@
         edges,
         scalars=1,
     )
-    pieces = lax.all_to_all(pieces, LON, 0, 0, tiled=True)
+    pieces = lax.all_to_all(pieces, LON, 0, 0, tiled=True, axis_index_groups=from_far(tiles, tiles // 2))
     pooled, sums = call(
         conv_kernel,
         "conv",
@@ -308,11 +316,13 @@
             pltpu.VMEM((channels * pool_rows, LANES), F32),
         ],
     )
-    sums = lax.all_to_all(sums, PLANE, 0, 0, tiled=True)
-    sums = call(sum_kernel, "sum_plane", [((lax.axis_size("z"), 8, LANES), F32)], sums)
-    sums = lax.all_to_all(sums, "z", 0, 0, tiled=True)
+    plane = from_far(members, members // 2 + lax.axis_size("y") // 2 * lax.axis_size("c"))
+    depth = lax.axis_size("z")
+    sums = lax.all_to_all(sums, PLANE, 0, 0, tiled=True, axis_index_groups=plane)
+    sums = call(sum_kernel, "sum_plane", [((depth, 8, LANES), F32)], sums)
+    sums = lax.all_to_all(sums, "z", 0, 0, tiled=True, axis_index_groups=from_far(depth, depth // 2))
     sums = call(sum_kernel, "sum_z", [((members, 8, LANES), F32)], sums)
-    sums = lax.all_to_all(sums, PLANE, 0, 0, tiled=True)
+    sums = lax.all_to_all(sums, PLANE, 0, 0, tiled=True, axis_index_groups=plane)
     grad_weight, grad_bias, grad_land, pooled = call(
         unpack_kernel,
         "unpack",

time: 94.4 us -> 87 us (0.922)
  blocking collectives: 84.3 us -> 76.9 us
    all_to_all x4, blocking collectives: 79.9 us -> 72.5 us  [the longest x1 31.8 us: local(): lax.all_to_all(pieces, LON, 0, 0, tiled=True, axis_index_groups=from_far(...]
where the time goes in v4:
time: 87 us; the launch traced here: 86.7 us
  blocking collectives  76.9 us (88%)
  starting transfers between devices  4.59 us (5%)
  Pallas kernels  4.52 us (5%)
    all_to_all x1, blocking collectives, local(): lax.all_to_all(pieces, LON, 0, 0, tiled=True, axis_index_groups=from_far(...  31.8 us
    all_to_all x2, blocking collectives, local(): lax.all_to_all(sums, PLANE, 0, 0, tiled=True, axis_index_groups=plane)  24.3 us
    all_to_all x1, blocking collectives, local(): lax.all_to_all(sums, 'z', 0, 0, tiled=True, axis_index_groups=from_far(de...  16.4 us
    ppermute x1, starting transfers between devices, local(): outer = lax.ppermute(outer, LAT, swap)  4.59 us
    pallas_call x7, Pallas kernels, call(): pl.pallas_call(kernel, name=name, out_shape=shapes[0] if single else shap...  4.52 us
    all_gather x1, blocking collectives, local(): inner = lax.all_gather(inner, 'c', axis=0, tiled=True)  4.45 us
  transfers between devices with their start and end apart: 1, of which 0 were waited for; matrix products, arithmetic and copies ran while one was open for 0% of the time, Pallas kernels for 0%

profile of v4, /device:TPU:1, one launch (start us, length us, event | category | flops | bytes accessed | tf_op | source)
XLA Modules:
  0.0 86.7 jit_solution(9132244523928331869)
XLA Ops:
  0.6 1.2 %first.1 = (bf16[16,8192]{1,0:T(8,128)(2,1)S(1)}, bf16[288,64]{1,0:T(8,128)(2,1)S(1)}, f32[1,64]{1,0:T(1,128)S(1)}, f32[1,64]{1,0:T(1,128)S(1)}, s32[16,256]{1,0...) custom-call(s32[1]{0:T(128)} %bitcast.core_ref, ...), custom_call_target="tpu_custom_call" | custom-call | tf_op jit(solution)/shard_map/first/pallas_call | solution.py:234
  1.8 4.6 %collective-permute-start = (bf16[1,8192]{1,0:T(2,128)(2,1)S(1)}, bf16[1,8192]{1,0:T(2,128)(2,1)S(1)}, u32[]{:S(2)}, u32[]{:S(2)}) collective-permute-start(bf16[1,8192]{1,0:T(2,128)(2,1)S(1)} %get-tuple-element.32), channel_id=1, source_target_pairs={{32,64},{64,32},{96,128},{128,96},{160,192},{192,160},{224,256},{2... | collective-permute-start | bytes 49160 | tf_op jit(solution)/shard_map/ppermute | solution.py:274
  6.4 4.5 %all_gather.3.after_ref.inner_ref = f32[128,128]{1,0:T(8,128)S(1)} all-gather(f32[64,128]{1,0:T(8,128)S(1)} %get-tuple-element.33), channel_id=1, replica_groups=mesh['xh'=2,'y'=4,'c'=2,'z'=16,'xl'=2] {'c'}, dimensions={0}, use_global_device_ids=true | all-gather | bytes 98304 | tf_op jit(solution)/shard_map/all_gather | solution.py:275
  10.9 0.3 prepare.1
  11.2 0.0 collective-permute-done.outer_ref
  11.2 0.3 pack.1
  11.5 31.8 %all_to_all.20.r_ref = bf16[32,40,128]{2,1,0:T(8,128)(2,1)S(1)} all-to-all(bf16[32,40,128]{2,1,0:T(8,128)(2,1)S(1)} %pack.1), channel_id=1, replica_groups={{16,17,18,19,20,21,22,23,24,25,26,27,28,29,30,31,0,1,2,3,4,5,6,7,8,9,10..., dimensions={0} | all-to-all | bytes 655360 | tf_op jit(solution)/shard_map/all_to_all | solution.py:304
  43.3 1.9 %conv.1 = (bf16[64,8,128]{2,1,0:T(8,128)(2,1)S(1)}, f32[32,8,128]{2,1,0:T(8,128)S(1)}) custom-call(bf16[32,40,128]{2,1,0:T(8,128)(2,1)S(1)} %all_to_all.20.r_ref, bf16[128,384]{1,0:T(8,128)(2,1)S(1)} %get-tuple-element.47.w_ref, f32[64,256]{1,0:T(8,128)S(1)} %get-tuple-element.48.bias_ref, f32[64,256]{1,0:T(8,128)S(1)} %get-tuple-element.49.land_ref, ...), custom_call_target="tpu_custom_call" | custom-call | tf_op jit(solution)/shard_map/conv/pallas_call | solution.py:234
  45.2 12.8 %all_to_all.21.x_ref = f32[32,8,128]{2,1,0:T(8,128)S(1)} all-to-all(f32[32,8,128]{2,1,0:T(8,128)S(1)} %get-tuple-element.52), channel_id=1, replica_groups={{384,416,448,480,257,289,321,353,385,417,449,481,0,32,64,96,128,160,192..., dimensions={0} | all-to-all | bytes 262144 | tf_op jit(solution)/shard_map/all_to_all | solution.py:321
  58.1 16.4 %all_to_all.22.x_ref = f32[16,8,128]{2,1,0:T(8,128)S(1)} all-to-all(f32[16,8,128]{2,1,0:T(8,128)S(1)} %sum_plane.1), channel_id=1, replica_groups={{16,18,20,22,24,26,28,30,0,2,4,6,8,10,12,14},{17,19,21,23,25,27,29,31,1..., dimensions={0} | all-to-all | bytes 131072 | tf_op jit(solution)/shard_map/all_to_all | solution.py:323
  74.5 11.5 %all_to_all.23.x_ref = f32[32,8,128]{2,1,0:T(8,128)S(1)} all-to-all(f32[32,8,128]{2,1,0:T(8,128)S(1)} %sum_z.1), channel_id=1, replica_groups={{384,416,448,480,257,289,321,353,385,417,449,481,0,32,64,96,128,160,192..., dimensions={0} | all-to-all | bytes 262144 | tf_op jit(solution)/shard_map/all_to_all | solution.py:325
  85.9 0.8 unpack.1
  (2 shorter events, 0.1 us)
Async XLA Ops:
  1.8 9.4 %collective-permute-start = (bf16[1,8192]{1,0:T(2,128)(2,1)S(1)}, bf16[1,8192]{1,0:T(2,128)(2,1)S(1)}, u32[]{:S(2)}, u32[]{:S(2)}) collective-permute-start(bf16[1,8192]{1,0:T(2,128)(2,1)S(1)} %get-tuple-element.32), channel_id=1, source_target_pairs={{32,64},{64,32},{96,128},{128,96},{160,192},{192,160},{224,256},{2... | collective-permute-start | bytes 49160 | tf_op jit(solution)/shard_map/ppermute | solution.py:274

commit v5 on v4

--- a/solution.py
+++ b/solution.py
@@ -30,7 +30,11 @@
 
 
 def turned(index, count):
-    return (index + count // 2) % count
+    return (index - far_lon(count)) % count
+
+
+def far_lon(count):
+    return count // 2 + 2
 
 
 def from_far(count, start):
@@ -301,7 +305,7 @@
         edges,
         scalars=1,
     )
-    pieces = lax.all_to_all(pieces, LON, 0, 0, tiled=True, axis_index_groups=from_far(tiles, tiles // 2))
+    pieces = lax.all_to_all(pieces, LON, 0, 0, tiled=True, axis_index_groups=from_far(tiles, far_lon(tiles)))
     pooled, sums = call(
         conv_kernel,
         "conv",
@@ -316,7 +320,7 @@
             pltpu.VMEM((channels * pool_rows, LANES), F32),
         ],
     )
-    plane = from_far(members, members // 2 + lax.axis_size("y") // 2 * lax.axis_size("c"))
+    plane = from_far(members, members // 2 + lax.axis_size("y") // 2 * lax.axis_size("c") + 1)
     depth = lax.axis_size("z")
     sums = lax.all_to_all(sums, PLANE, 0, 0, tiled=True, axis_index_groups=plane)
     sums = call(sum_kernel, "sum_plane", [((depth, 8, LANES), F32)], sums)

time: 87 us -> 85.5 us (0.983)
  blocking collectives: 76.9 us -> 75.5 us
    all_to_all x1, blocking collectives: 16.4 us -> 14.7 us  [local(): lax.all_to_all(sums, 'z', 0, 0, tiled=True, axis_index_groups=from_far(de...]
where the time goes in v5:
time: 85.5 us; the launch traced here: 85.3 us
  blocking collectives  75.5 us (88%)
  starting transfers between devices  4.59 us (5%)
  Pallas kernels  4.51 us (5%)
    all_to_all x1, blocking collectives, local(): lax.all_to_all(pieces, LON, 0, 0, tiled=True, axis_index_groups=from_far(...  31.8 us
    all_to_all x2, blocking collectives, local(): lax.all_to_all(sums, PLANE, 0, 0, tiled=True, axis_index_groups=plane)  24.5 us
    all_to_all x1, blocking collectives, local(): lax.all_to_all(sums, 'z', 0, 0, tiled=True, axis_index_groups=from_far(de...  14.7 us
    ppermute x1, starting transfers between devices, local(): outer = lax.ppermute(outer, LAT, swap)  4.59 us
    pallas_call x7, Pallas kernels, call(): pl.pallas_call(kernel, name=name, out_shape=shapes[0] if single else shap...  4.51 us
    all_gather x1, blocking collectives, local(): inner = lax.all_gather(inner, 'c', axis=0, tiled=True)  4.45 us
  transfers between devices with their start and end apart: 1, of which 0 were waited for; matrix products, arithmetic and copies ran while one was open for 0% of the time, Pallas kernels for 0%

profile of v5, /device:TPU:1, one launch (start us, length us, event | category | flops | bytes accessed | tf_op | source)
XLA Modules:
  0.0 85.3 jit_solution(12773623438799216530)
XLA Ops:
  0.6 1.2 %first.1 = (bf16[16,8192]{1,0:T(8,128)(2,1)S(1)}, bf16[288,64]{1,0:T(8,128)(2,1)S(1)}, f32[1,64]{1,0:T(1,128)S(1)}, f32[1,64]{1,0:T(1,128)S(1)}, s32[16,256]{1,0...) custom-call(s32[1]{0:T(128)} %bitcast.core_ref, ...), custom_call_target="tpu_custom_call" | custom-call | tf_op jit(solution)/shard_map/first/pallas_call | solution.py:238
  1.8 4.6 %collective-permute-start = (bf16[1,8192]{1,0:T(2,128)(2,1)S(1)}, bf16[1,8192]{1,0:T(2,128)(2,1)S(1)}, u32[]{:S(2)}, u32[]{:S(2)}) collective-permute-start(bf16[1,8192]{1,0:T(2,128)(2,1)S(1)} %get-tuple-element.32), channel_id=1, source_target_pairs={{32,64},{64,32},{96,128},{128,96},{160,192},{192,160},{224,256},{2... | collective-permute-start | bytes 49160 | tf_op jit(solution)/shard_map/ppermute | solution.py:278
  6.4 4.5 %all_gather.3.after_ref.inner_ref = f32[128,128]{1,0:T(8,128)S(1)} all-gather(f32[64,128]{1,0:T(8,128)S(1)} %get-tuple-element.33), channel_id=1, replica_groups=mesh['xh'=2,'y'=4,'c'=2,'z'=16,'xl'=2] {'c'}, dimensions={0}, use_global_device_ids=true | all-gather | bytes 98304 | tf_op jit(solution)/shard_map/all_gather | solution.py:279
  10.9 0.3 prepare.1
  11.2 0.0 collective-permute-done.outer_ref
  11.2 0.3 pack.1
  11.5 31.8 %all_to_all.20.r_ref = bf16[32,40,128]{2,1,0:T(8,128)(2,1)S(1)} all-to-all(bf16[32,40,128]{2,1,0:T(8,128)(2,1)S(1)} %pack.1), channel_id=1, replica_groups={{18,19,20,21,22,23,24,25,26,27,28,29,30,31,0,1,2,3,4,5,6,7,8,9,10,11,12..., dimensions={0} | all-to-all | bytes 655360 | tf_op jit(solution)/shard_map/all_to_all | solution.py:308
  43.3 1.9 %conv.1 = (bf16[64,8,128]{2,1,0:T(8,128)(2,1)S(1)}, f32[32,8,128]{2,1,0:T(8,128)S(1)}) custom-call(bf16[32,40,128]{2,1,0:T(8,128)(2,1)S(1)} %all_to_all.20.r_ref, bf16[128,384]{1,0:T(8,128)(2,1)S(1)} %get-tuple-element.47.w_ref, f32[64,256]{1,0:T(8,128)S(1)} %get-tuple-element.48.bias_ref, f32[64,256]{1,0:T(8,128)S(1)} %get-tuple-element.49.land_ref, ...), custom_call_target="tpu_custom_call" | custom-call | tf_op jit(solution)/shard_map/conv/pallas_call | solution.py:238
  45.2 12.5 %all_to_all.21.x_ref = f32[32,8,128]{2,1,0:T(8,128)S(1)} all-to-all(f32[32,8,128]{2,1,0:T(8,128)S(1)} %get-tuple-element.52), channel_id=1, replica_groups={{416,448,480,257,289,321,353,385,417,449,481,0,32,64,96,128,160,192,224..., dimensions={0} | all-to-all | bytes 262144 | tf_op jit(solution)/shard_map/all_to_all | solution.py:325
  57.8 14.7 %all_to_all.22.x_ref = f32[16,8,128]{2,1,0:T(8,128)S(1)} all-to-all(f32[16,8,128]{2,1,0:T(8,128)S(1)} %sum_plane.1), channel_id=1, replica_groups={{16,18,20,22,24,26,28,30,0,2,4,6,8,10,12,14},{17,19,21,23,25,27,29,31,1..., dimensions={0} | all-to-all | bytes 131072 | tf_op jit(solution)/shard_map/all_to_all | solution.py:327
  72.4 12.0 %all_to_all.23.x_ref = f32[32,8,128]{2,1,0:T(8,128)S(1)} all-to-all(f32[32,8,128]{2,1,0:T(8,128)S(1)} %sum_z.1), channel_id=1, replica_groups={{416,448,480,257,289,321,353,385,417,449,481,0,32,64,96,128,160,192,224..., dimensions={0} | all-to-all | bytes 262144 | tf_op jit(solution)/shard_map/all_to_all | solution.py:329
  84.5 0.8 unpack.1
  (2 shorter events, 0.1 us)
Async XLA Ops:
  1.8 9.4 %collective-permute-start = (bf16[1,8192]{1,0:T(2,128)(2,1)S(1)}, bf16[1,8192]{1,0:T(2,128)(2,1)S(1)}, u32[]{:S(2)}, u32[]{:S(2)}) collective-permute-start(bf16[1,8192]{1,0:T(2,128)(2,1)S(1)} %get-tuple-element.32), channel_id=1, source_target_pairs={{32,64},{64,32},{96,128},{128,96},{160,192},{192,160},{224,256},{2... | collective-permute-start | bytes 49160 | tf_op jit(solution)/shard_map/ppermute | solution.py:278

commit v6 on v5

--- a/solution.py
+++ b/solution.py
@@ -122,8 +122,8 @@
     mask_out[...] = mask_ref[...].astype(F32)
     spread = (iota((LANES, COLS), 1) // 2 == iota((LANES, COLS), 0)).astype(F32).astype(BF16)
     wide = jnp.dot(cot_ref[...].reshape(channels * pool_rows, LANES), spread, preferred_element_type=F32) * factor
-    wide0[...] = wide[:, :LANES]
-    wide1[...] = wide[:, LANES:]
+    wide0[0 : channels * pool_rows, :] = wide[:, :LANES]
+    wide1[0 : channels * pool_rows, :] = wide[:, LANES:]
     for p in range(pool_rows):
         here = pl.ds(p, channels, stride=pool_rows)
         wide_out[p] = jnp.concatenate([wide0[here, :], wide1[here, :]], axis=1)
@@ -203,7 +203,8 @@
     sums_ref[used] = jnp.broadcast_to(jnp.concatenate([across(grad_b), across(grad_l)], axis=1), (8, LANES))
     sums_ref[used + 1 :] = jnp.zeros((sums_ref.shape[0] - used - 1, 8, LANES), F32)
     pair = (iota((COLS, LANES), 0) == 2 * iota((COLS, LANES), 1)).astype(F32).astype(BF16)
-    halves = [((act[...] + pltpu.roll(act[...], LANES - 1, 1)) * 0.25).astype(BF16) for act in (act0, act1)]
+    sums = [act[0 : channels * pool_rows, :] for act in (act0, act1)]
+    halves = [((two + pltpu.roll(two, LANES - 1, 1)) * 0.25).astype(BF16) for two in sums]
     pooled = jnp.dot(jnp.concatenate(halves, axis=1), pair, preferred_element_type=F32)
     pooled_ref[...] = pooled.astype(BF16).reshape(pooled_ref.shape)
 
@@ -290,7 +291,7 @@
         ],
         *held[1:],
         after,
-        scratch=[pltpu.VMEM((channels * pool_rows, LANES), F32)] * 2,
+        scratch=[pltpu.VMEM(((channels + 1) * pool_rows, LANES), F32)] * 2,
         places=[VMEM] * 5 + [ANY],
     )
     outer, inner, prepared = lax.optimization_barrier((outer, inner, prepared))
@@ -313,11 +314,11 @@
         pieces,
         *prepared,
         scratch=[
-            pltpu.VMEM((in_fields * PIECE, LANES), F32),
+            pltpu.VMEM(((in_fields + 1) * PIECE, LANES), F32),
             pltpu.VMEM((ROWS + 2, 3 * in_fields, COLS), BF16),
             pltpu.VMEM((pool_rows, 2 * channels, COLS), BF16),
-            pltpu.VMEM((channels * pool_rows, LANES), F32),
-            pltpu.VMEM((channels * pool_rows, LANES), F32),
+            pltpu.VMEM(((channels + 1) * pool_rows, LANES), F32),
+            pltpu.VMEM(((channels + 1) * pool_rows, LANES), F32),
         ],
     )
     plane = from_far(members, members // 2 + lax.axis_size("y") // 2 * lax.axis_size("c") + 1)

time: 85.5 us -> 85.5 us (level)
  no operation moved by 1% of the time
where the time goes in v6:
time: 85.5 us; the launch traced here: 85.3 us
  blocking collectives  75.5 us (88%)
  starting transfers between devices  4.59 us (5%)
  Pallas kernels  4.52 us (5%)
    all_to_all x1, blocking collectives, local(): lax.all_to_all(pieces, LON, 0, 0, tiled=True, axis_index_groups=from_far(...  31.8 us
    all_to_all x2, blocking collectives, local(): lax.all_to_all(sums, PLANE, 0, 0, tiled=True, axis_index_groups=plane)  24.5 us
    all_to_all x1, blocking collectives, local(): lax.all_to_all(sums, 'z', 0, 0, tiled=True, axis_index_groups=from_far(de...  14.7 us
    ppermute x1, starting transfers between devices, local(): outer = lax.ppermute(outer, LAT, swap)  4.59 us
    pallas_call x7, Pallas kernels, call(): pl.pallas_call(kernel, name=name, out_shape=shapes[0] if single else shap...  4.52 us
    all_gather x1, blocking collectives, local(): inner = lax.all_gather(inner, 'c', axis=0, tiled=True)  4.45 us
  transfers between devices with their start and end apart: 1, of which 0 were waited for; matrix products, arithmetic and copies ran while one was open for 0% of the time, Pallas kernels for 0%

profile of v6, /device:TPU:1, one launch (start us, length us, event | category | flops | bytes accessed | tf_op | source)
XLA Modules:
  0.0 85.3 jit_solution(2323389477108031420)
XLA Ops:
  0.6 1.2 %first.1 = (bf16[16,8192]{1,0:T(8,128)(2,1)S(1)}, bf16[288,64]{1,0:T(8,128)(2,1)S(1)}, f32[1,64]{1,0:T(1,128)S(1)}, f32[1,64]{1,0:T(1,128)S(1)}, s32[16,256]{1,0...) custom-call(s32[1]{0:T(128)} %bitcast.core_ref, ...), custom_call_target="tpu_custom_call" | custom-call | tf_op jit(solution)/shard_map/first/pallas_call | solution.py:239
  1.8 4.6 %collective-permute-start = (bf16[1,8192]{1,0:T(2,128)(2,1)S(1)}, bf16[1,8192]{1,0:T(2,128)(2,1)S(1)}, u32[]{:S(2)}, u32[]{:S(2)}) collective-permute-start(bf16[1,8192]{1,0:T(2,128)(2,1)S(1)} %get-tuple-element.32), channel_id=1, source_target_pairs={{32,64},{64,32},{96,128},{128,96},{160,192},{192,160},{224,256},{2... | collective-permute-start | bytes 49160 | tf_op jit(solution)/shard_map/ppermute | solution.py:279
  6.4 4.5 %all_gather.3.after_ref.inner_ref = f32[128,128]{1,0:T(8,128)S(1)} all-gather(f32[64,128]{1,0:T(8,128)S(1)} %get-tuple-element.33), channel_id=1, replica_groups=mesh['xh'=2,'y'=4,'c'=2,'z'=16,'xl'=2] {'c'}, dimensions={0}, use_global_device_ids=true | all-gather | bytes 98304 | tf_op jit(solution)/shard_map/all_gather | solution.py:280
  10.9 0.3 prepare.1
  11.2 0.0 collective-permute-done.outer_ref
  11.2 0.3 pack.1
  11.5 31.8 %all_to_all.20.r_ref = bf16[32,40,128]{2,1,0:T(8,128)(2,1)S(1)} all-to-all(bf16[32,40,128]{2,1,0:T(8,128)(2,1)S(1)} %pack.1), channel_id=1, replica_groups={{18,19,20,21,22,23,24,25,26,27,28,29,30,31,0,1,2,3,4,5,6,7,8,9,10,11,12..., dimensions={0} | all-to-all | bytes 655360 | tf_op jit(solution)/shard_map/all_to_all | solution.py:309
  43.3 1.9 %conv.1 = (bf16[64,8,128]{2,1,0:T(8,128)(2,1)S(1)}, f32[32,8,128]{2,1,0:T(8,128)S(1)}) custom-call(bf16[32,40,128]{2,1,0:T(8,128)(2,1)S(1)} %all_to_all.20.r_ref, bf16[128,384]{1,0:T(8,128)(2,1)S(1)} %get-tuple-element.47.w_ref, f32[64,256]{1,0:T(8,128)S(1)} %get-tuple-element.48.bias_ref, f32[64,256]{1,0:T(8,128)S(1)} %get-tuple-element.49.land_ref, ...), custom_call_target="tpu_custom_call" | custom-call | tf_op jit(solution)/shard_map/conv/pallas_call | solution.py:239
  45.2 12.5 %all_to_all.21.x_ref = f32[32,8,128]{2,1,0:T(8,128)S(1)} all-to-all(f32[32,8,128]{2,1,0:T(8,128)S(1)} %get-tuple-element.52), channel_id=1, replica_groups={{416,448,480,257,289,321,353,385,417,449,481,0,32,64,96,128,160,192,224..., dimensions={0} | all-to-all | bytes 262144 | tf_op jit(solution)/shard_map/all_to_all | solution.py:326
  57.8 14.7 %all_to_all.22.x_ref = f32[16,8,128]{2,1,0:T(8,128)S(1)} all-to-all(f32[16,8,128]{2,1,0:T(8,128)S(1)} %sum_plane.1), channel_id=1, replica_groups={{16,18,20,22,24,26,28,30,0,2,4,6,8,10,12,14},{17,19,21,23,25,27,29,31,1..., dimensions={0} | all-to-all | bytes 131072 | tf_op jit(solution)/shard_map/all_to_all | solution.py:328
  72.4 12.0 %all_to_all.23.x_ref = f32[32,8,128]{2,1,0:T(8,128)S(1)} all-to-all(f32[32,8,128]{2,1,0:T(8,128)S(1)} %sum_z.1), channel_id=1, replica_groups={{416,448,480,257,289,321,353,385,417,449,481,0,32,64,96,128,160,192,224..., dimensions={0} | all-to-all | bytes 262144 | tf_op jit(solution)/shard_map/all_to_all | solution.py:330
  84.5 0.8 unpack.1
  (2 shorter events, 0.1 us)
Async XLA Ops:
  1.8 9.4 %collective-permute-start = (bf16[1,8192]{1,0:T(2,128)(2,1)S(1)}, bf16[1,8192]{1,0:T(2,128)(2,1)S(1)}, u32[]{:S(2)}, u32[]{:S(2)}) collective-permute-start(bf16[1,8192]{1,0:T(2,128)(2,1)S(1)} %get-tuple-element.32), channel_id=1, source_target_pairs={{32,64},{64,32},{96,128},{128,96},{160,192},{192,160},{224,256},{2... | collective-permute-start | bytes 49160 | tf_op jit(solution)/shard_map/ppermute | solution.py:279

commit v7 on v6

--- a/solution.py
+++ b/solution.py
@@ -47,33 +47,26 @@
     return LANES - 1, (tile + 1) % tiles
 
 
-def pack_kernel(tiles, core_ref, x_ref, outer_ref, inner_ref, edges_ref, out_ref):
+def pack_kernel(tiles, core_ref, x_ref, outer_ref, inner_ref, columns_ref, out_ref):
     first = core_ref[0] == 0
     rows8 = iota((8, LANES), 0)
-    lanes = iota((8, LANES), 1)
-    beside = jnp.zeros((8, LANES), F32)
-    tails = []
+    last_lane = iota((1, LANES), 1) == LANES - 1
+    tops, bottoms = [], []
+    for k in range(2 * tiles):
+        at = pl.ds(k * LANES, LANES)
+        half = k % 2
+        out_ref[turned(k // 2, tiles), half * ROWS : (half + 1) * ROWS, :] = x_ref[:, at]
+        outer = outer_ref[:, at].astype(F32)
+        tops.append(jnp.where(first, outer, inner_ref[k : k + 1, :]))
+        bottoms.append(jnp.where(first, inner_ref[2 * tiles + k : 2 * tiles + k + 1, :], outer))
     for tile in range(tiles):
-        for half in range(2):
-            k = 2 * tile + half
-            at = pl.ds(k * LANES, LANES)
-            out_ref[turned(tile, tiles), half * ROWS : (half + 1) * ROWS, :] = x_ref[:, at]
-            outer = outer_ref[:, at].astype(F32)
-            top = jnp.where(first, outer, inner_ref[k : k + 1, :])
-            bottom = jnp.where(first, inner_ref[2 * tiles + k : 2 * tiles + k + 1, :], outer)
-            tails.append((top, bottom))
-            halo = jnp.where(rows8 == 0, top, jnp.where(rows8 == 1, bottom, 0.0))
-            source, target = edge_lanes(tiles, tile, half)
-            beside = jnp.where(lanes == target, pltpu.roll(halo, (target - source) % LANES, 1), beside)
-    square = jnp.concatenate([edges_ref[...], beside, jnp.zeros((LANES - ROWS - 8, LANES), F32)], axis=0).T
-    columns = square[:tiles] + pltpu.roll(square[64 : 64 + tiles], 64, 1)
-    for tile in range(tiles):
-        (top0, bottom0), (top1, bottom1) = tails[2 * tile : 2 * tile + 2]
-        tail = jnp.where(rows8 == 0, top0, 0.0)
-        tail = jnp.where(rows8 == 1, top1, tail)
-        tail = jnp.where(rows8 == 2, bottom0, tail)
-        tail = jnp.where(rows8 == 3, bottom1, tail)
-        tail = jnp.where(rows8 == 4, columns[tile : tile + 1], tail)
+        k = 2 * tile
+        before, behind = (k - 1) % (2 * tiles), (k + 2) % (2 * tiles)
+        rows = [tops[k], tops[k + 1], bottoms[k], bottoms[k + 1], columns_ref[tile : tile + 1, :]]
+        rows += [jnp.where(last_lane, halo[before], halo[behind]) for halo in (tops, bottoms)]
+        tail = jnp.zeros((8, LANES), F32)
+        for row, values in enumerate(rows):
+            tail = jnp.where(rows8 == row, values, tail)
         out_ref[turned(tile, tiles), 2 * ROWS : PIECE, :] = tail.astype(BF16)
 
 
@@ -81,35 +74,42 @@
     return jnp.sum(jnp.where(iota((count, count), 0) == iota((count, count), 1), row, 0.0), axis=1, keepdims=True)
 
 
-def edges_of(tiles, first, x_ref, outer_ref, inner_ref, edges_ref):
-    lanes = iota((ROWS, LANES), 1)
-    edges = jnp.zeros((ROWS, LANES), F32)
+def edges_of(tiles, first, x_ref, outer_ref, inner_ref):
     for k in range(2 * tiles):
         at = pl.ds(k * LANES, LANES)
         block = x_ref[:, at].astype(F32)
         top, bottom = block[0:1], block[ROWS - 1 : ROWS]
         outer_ref[:, at] = jnp.where(first, top, bottom).astype(BF16)
         inner_ref[k : k + 1, :] = jnp.where(first, bottom, top)
+
+
+def columns_of(tiles, x_ref):
+    lanes = iota((ROWS, LANES), 1)
+    edges = jnp.zeros((ROWS, LANES), F32)
+    for k in range(2 * tiles):
+        block = x_ref[:, pl.ds(k * LANES, LANES)].astype(F32)
         source, target = edge_lanes(tiles, k // 2, k % 2)
         edges = jnp.where(lanes == target, pltpu.roll(block, (target - source) % LANES, 1), edges)
-    edges_ref[...] = edges
+    square = jnp.concatenate([edges, jnp.zeros((LANES - ROWS, LANES), F32)], axis=0).T
+    return square[:tiles] + pltpu.roll(square[64 : 64 + tiles], 64, 1)
 
 
 def first_kernel(
-    tiles, core_ref, x_in, w_in, bias_in, land_in, mask_in, cot_in, x_ref, w_ref, bias_ref, land_ref, mask_ref, cot_ref, outer_ref, inner_ref, edges_ref, sems
+    tiles, core_ref, x_in, w_in, bias_in, land_in, mask_in, cot_in, x_ref, w_ref, bias_ref, land_ref, mask_ref, cot_ref, outer_ref, inner_ref, sems
 ):
     pairs = [(x_in, x_ref), (cot_in, cot_ref), (w_in, w_ref), (bias_in, bias_ref), (land_in, land_ref), (mask_in, mask_ref)]
     copies = [pltpu.make_async_copy(source, target, sems.at[k]) for k, (source, target) in enumerate(pairs)]
     for copy in copies:
         copy.start()
     copies[0].wait()
-    edges_of(tiles, core_ref[0] == 0, x_ref, outer_ref, inner_ref, edges_ref)
+    edges_of(tiles, core_ref[0] == 0, x_ref, outer_ref, inner_ref)
     for copy in copies[1:]:
         copy.wait()
 
 
-def prepare_kernel(factor, w_ref, bias_ref, land_ref, mask_ref, cot_ref, after_ref, w_out, bias_out, land_out, mask_out, wide_out, wide0, wide1):
+def prepare_kernel(tiles, factor, x_ref, w_ref, bias_ref, land_ref, mask_ref, cot_ref, after_ref, columns_out, w_out, bias_out, land_out, mask_out, wide_out, wide0, wide1):
     del after_ref
+    columns_out[...] = columns_of(tiles, x_ref)
     taps, channels = w_ref.shape
     pool_rows = ROWS // 2
     weight = w_ref[...].astype(F32).T
@@ -145,20 +145,20 @@
     last_lane = iota((fields, LANES), 1) == LANES - 1
     for r in range(ROWS + 2):
         if r == 0:
-            k0, k1, lane = 32, 33, 16
+            k0, k1, sides, left, right = 32, 33, take(37), LANES - 1, 0
         elif r == ROWS + 1:
-            k0, k1, lane = 34, 35, 17
+            k0, k1, sides, left, right = 34, 35, take(38), LANES - 1, 0
         else:
-            k0, k1, lane = r - 1, ROWS + r - 1, r - 1
+            k0, k1, sides, left, right = r - 1, ROWS + r - 1, columns, r - 1, 63 + r
         a, b = take(k0), take(k1)
         up_a, up_b = pltpu.roll(a, 1, 1), pltpu.roll(b, 1, 1)
         down_a, down_b = pltpu.roll(a, LANES - 1, 1), pltpu.roll(b, LANES - 1, 1)
-        patch_ref[r, 0:fields, :LANES] = jnp.where(first_lane, columns[:, lane : lane + 1], up_a).astype(BF16)
+        patch_ref[r, 0:fields, :LANES] = jnp.where(first_lane, sides[:, left : left + 1], up_a).astype(BF16)
         patch_ref[r, 0:fields, LANES:] = jnp.where(first_lane, up_a, up_b).astype(BF16)
         patch_ref[r, fields : 2 * fields, :LANES] = a.astype(BF16)
         patch_ref[r, fields : 2 * fields, LANES:] = b.astype(BF16)
         patch_ref[r, 2 * fields :, :LANES] = jnp.where(last_lane, down_b, down_a).astype(BF16)
-        patch_ref[r, 2 * fields :, LANES:] = jnp.where(last_lane, columns[:, 64 + lane : 65 + lane], down_b).astype(BF16)
+        patch_ref[r, 2 * fields :, LANES:] = jnp.where(last_lane, sides[:, right : right + 1], down_b).astype(BF16)
 
     root = math.sqrt(2.0 / math.pi)
     weight = w_ref[...]
@@ -265,11 +265,11 @@
         land_mask,
         cotangent,
     )
-    *held, outer, inner, edges = call(
+    *held, outer, inner = call(
         functools.partial(first_kernel, tiles),
         "first",
         [(array.shape, array.dtype) for array in given]
-        + [((1, columns), BF16), ((columns // LANES, LANES), F32), ((ROWS, LANES), F32)],
+        + [((1, columns), BF16), ((columns // LANES, LANES), F32)],
         core,
         *(pltpu.with_memory_space_constraint(array, pltpu.HBM) for array in given),
         scratch=[pltpu.SemaphoreType.DMA((6,))],
@@ -279,22 +279,23 @@
     outer = lax.ppermute(outer, LAT, swap)
     inner = lax.all_gather(inner, "c", axis=0, tiled=True)
     after = inner
-    prepared = call(
-        functools.partial(prepare_kernel, factor),
+    beside, *prepared = call(
+        functools.partial(prepare_kernel, tiles, factor),
         "prepare",
         [
+            ((tiles, LANES), F32),
             ((2 * channels, 4 * taps // 3), BF16),
             ((channels, COLS), F32),
             ((channels, COLS), F32),
             ((ROWS, COLS), F32),
             ((pool_rows, channels, COLS), F32),
         ],
-        *held[1:],
+        *held,
         after,
         scratch=[pltpu.VMEM(((channels + 1) * pool_rows, LANES), F32)] * 2,
-        places=[VMEM] * 5 + [ANY],
-    )
-    outer, inner, prepared = lax.optimization_barrier((outer, inner, prepared))
+        places=[VMEM] * 6 + [ANY],
+    )
+    outer, inner, beside, prepared = lax.optimization_barrier((outer, inner, beside, prepared))
     pieces = call(
         functools.partial(pack_kernel, tiles),
         "pack",
@@ -303,7 +304,7 @@
         held[0],
         outer,
         inner,
-        edges,
+        beside,
         scalars=1,
     )
     pieces = lax.all_to_all(pieces, LON, 0, 0, tiled=True, axis_index_groups=from_far(tiles, far_lon(tiles)))

time: 85.5 us -> 85.5 us (level)
  transfers between devices with their start and end apart: 1 -> 1, of which waited for: 0 -> 0; matrix products, arithmetic and copies ran while one was open for 0% -> 0% of each run, Pallas kernels for 0% -> 1%
where the time goes in v7:
time: 85.5 us; the launch traced here: 85.2 us
  blocking collectives  75.5 us (88%)
  starting transfers between devices  4.59 us (5%)
  Pallas kernels  4.43 us (5%)
    all_to_all x1, blocking collectives, local(): lax.all_to_all(pieces, LON, 0, 0, tiled=True, axis_index_groups=from_far(...  31.8 us
    all_to_all x2, blocking collectives, local(): lax.all_to_all(sums, PLANE, 0, 0, tiled=True, axis_index_groups=plane)  24.5 us
    all_to_all x1, blocking collectives, local(): lax.all_to_all(sums, 'z', 0, 0, tiled=True, axis_index_groups=from_far(de...  14.7 us
    ppermute x1, starting transfers between devices, local(): outer = lax.ppermute(outer, LAT, swap)  4.59 us
    all_gather x1, blocking collectives, local(): inner = lax.all_gather(inner, 'c', axis=0, tiled=True)  4.45 us
    pallas_call x7, Pallas kernels, call(): pl.pallas_call(kernel, name=name, out_shape=shapes[0] if single else shap...  4.43 us
  transfers between devices with their start and end apart: 1, of which 0 were waited for; matrix products, arithmetic and copies ran while one was open for 0% of the time, Pallas kernels for 1%

profile of v7, /device:TPU:1, one launch (start us, length us, event | category | flops | bytes accessed | tf_op | source)
XLA Modules:
  0.0 85.2 jit_solution(9100956172474845069)
XLA Ops:
  0.6 1.1 %first.1 = (bf16[16,8192]{1,0:T(8,128)(2,1)S(1)}, bf16[288,64]{1,0:T(8,128)(2,1)S(1)}, f32[1,64]{1,0:T(1,128)S(1)}, f32[1,64]{1,0:T(1,128)S(1)}, s32[16,256]{1,0...) custom-call(s32[1]{0:T(128)} %bitcast.core_ref, ...), custom_call_target="tpu_custom_call" | custom-call | tf_op jit(solution)/shard_map/first/pallas_call | solution.py:239
  1.7 4.6 %collective-permute-start = (bf16[1,8192]{1,0:T(2,128)(2,1)S(1)}, bf16[1,8192]{1,0:T(2,128)(2,1)S(1)}, u32[]{:S(2)}, u32[]{:S(2)}) collective-permute-start(bf16[1,8192]{1,0:T(2,128)(2,1)S(1)} %get-tuple-element.33), channel_id=1, source_target_pairs={{32,64},{64,32},{96,128},{128,96},{160,192},{192,160},{224,256},{2... | collective-permute-start | bytes 49160 | tf_op jit(solution)/shard_map/ppermute | solution.py:279
  6.3 4.5 %all_gather.3.after_ref.inner_ref = f32[128,128]{1,0:T(8,128)S(1)} all-gather(f32[64,128]{1,0:T(8,128)S(1)} %get-tuple-element.34), channel_id=1, replica_groups=mesh['xh'=2,'y'=4,'c'=2,'z'=16,'xl'=2] {'c'}, dimensions={0}, use_global_device_ids=true | all-gather | bytes 98304 | tf_op jit(solution)/shard_map/all_gather | solution.py:280
  10.8 0.5 prepare.1
  11.3 0.0 collective-permute-done.outer_ref
  11.3 0.1 pack.1
  11.4 31.8 %all_to_all.20.r_ref = bf16[32,40,128]{2,1,0:T(8,128)(2,1)S(1)} all-to-all(bf16[32,40,128]{2,1,0:T(8,128)(2,1)S(1)} %pack.1), channel_id=1, replica_groups={{18,19,20,21,22,23,24,25,26,27,28,29,30,31,0,1,2,3,4,5,6,7,8,9,10,11,12..., dimensions={0} | all-to-all | bytes 655360 | tf_op jit(solution)/shard_map/all_to_all | solution.py:310
  43.3 1.9 %conv.1 = (bf16[64,8,128]{2,1,0:T(8,128)(2,1)S(1)}, f32[32,8,128]{2,1,0:T(8,128)S(1)}) custom-call(bf16[32,40,128]{2,1,0:T(8,128)(2,1)S(1)} %all_to_all.20.r_ref, bf16[128,384]{1,0:T(8,128)(2,1)S(1)} %get-tuple-element.49.w_ref, f32[64,256]{1,0:T(8,128)S(1)} %get-tuple-element.50.bias_ref, f32[64,256]{1,0:T(8,128)S(1)} %get-tuple-element.51.land_ref, ...), custom_call_target="tpu_custom_call" | custom-call | tf_op jit(solution)/shard_map/conv/pallas_call | solution.py:239
  45.1 12.5 %all_to_all.21.x_ref = f32[32,8,128]{2,1,0:T(8,128)S(1)} all-to-all(f32[32,8,128]{2,1,0:T(8,128)S(1)} %get-tuple-element.54), channel_id=1, replica_groups={{416,448,480,257,289,321,353,385,417,449,481,0,32,64,96,128,160,192,224..., dimensions={0} | all-to-all | bytes 262144 | tf_op jit(solution)/shard_map/all_to_all | solution.py:327
  57.7 14.7 %all_to_all.22.x_ref = f32[16,8,128]{2,1,0:T(8,128)S(1)} all-to-all(f32[16,8,128]{2,1,0:T(8,128)S(1)} %sum_plane.1), channel_id=1, replica_groups={{16,18,20,22,24,26,28,30,0,2,4,6,8,10,12,14},{17,19,21,23,25,27,29,31,1..., dimensions={0} | all-to-all | bytes 131072 | tf_op jit(solution)/shard_map/all_to_all | solution.py:329
  72.4 12.0 %all_to_all.23.x_ref = f32[32,8,128]{2,1,0:T(8,128)S(1)} all-to-all(f32[32,8,128]{2,1,0:T(8,128)S(1)} %sum_z.1), channel_id=1, replica_groups={{416,448,480,257,289,321,353,385,417,449,481,0,32,64,96,128,160,192,224..., dimensions={0} | all-to-all | bytes 262144 | tf_op jit(solution)/shard_map/all_to_all | solution.py:331
  84.4 0.8 unpack.1
  (2 shorter events, 0.1 us)
Async XLA Ops:
  1.7 9.5 %collective-permute-start = (bf16[1,8192]{1,0:T(2,128)(2,1)S(1)}, bf16[1,8192]{1,0:T(2,128)(2,1)S(1)}, u32[]{:S(2)}, u32[]{:S(2)}) collective-permute-start(bf16[1,8192]{1,0:T(2,128)(2,1)S(1)} %get-tuple-element.33), channel_id=1, source_target_pairs={{32,64},{64,32},{96,128},{128,96},{160,192},{192,160},{224,256},{2... | collective-permute-start | bytes 49160 | tf_op jit(solution)/shard_map/ppermute | solution.py:279

commit v8 on v7

--- a/solution.py
+++ b/solution.py
@@ -210,7 +210,7 @@
 
 
 def sum_kernel(x_ref, out_ref):
-    out_ref[...] = jnp.broadcast_to(jnp.sum(x_ref[...], axis=0, keepdims=True), out_ref.shape)
+    out_ref[...] = jnp.broadcast_to(jnp.sum(x_ref[...], axis=0, keepdims=True).astype(out_ref.dtype), out_ref.shape)
 
 
 def unpack_kernel(x_ref, pooled_ref, weight_out, bias_out, land_out, pooled_out, weight_ref, rows_ref, sems):
@@ -219,9 +219,10 @@
     taps, channels = weight_ref.shape
     half_taps = taps // 2
     used = half_taps // 8
-    rows_ref[0:1, :] = x_ref[used, 0:1, :channels]
-    rows_ref[8:9, :] = x_ref[used, 0:1, channels:]
-    both = x_ref[0:used].reshape(half_taps, LANES)
+    sides = x_ref[used].astype(F32)
+    rows_ref[0:1, :] = sides[0:1, :channels]
+    rows_ref[8:9, :] = sides[0:1, channels:]
+    both = x_ref[0:used].astype(F32).reshape(half_taps, LANES)
     weight_ref[0:half_taps, :] = both[:, :channels]
     weight_ref[half_taps:, :] = both[:, channels:]
     pairs = ((weight_ref, weight_out), (rows_ref.at[0:1], bias_out), (rows_ref.at[8:9], land_out))
@@ -327,7 +328,7 @@
     sums = lax.all_to_all(sums, PLANE, 0, 0, tiled=True, axis_index_groups=plane)
     sums = call(sum_kernel, "sum_plane", [((depth, 8, LANES), F32)], sums)
     sums = lax.all_to_all(sums, "z", 0, 0, tiled=True, axis_index_groups=from_far(depth, depth // 2))
-    sums = call(sum_kernel, "sum_z", [((members, 8, LANES), F32)], sums)
+    sums = call(sum_kernel, "sum_z", [((members, 8, LANES), BF16)], sums)
     sums = lax.all_to_all(sums, PLANE, 0, 0, tiled=True, axis_index_groups=plane)
     grad_weight, grad_bias, grad_land, pooled = call(
         unpack_kernel,

time: 85.5 us -> 85 us (level)
  no operation moved by 1% of the time
where the time goes in v8:
time: 85 us; the launch traced here: 84.8 us
  blocking collectives  75.1 us (88%)
  starting transfers between devices  4.59 us (5%)
  Pallas kernels  4.42 us (5%)
    all_to_all x1, blocking collectives, local(): lax.all_to_all(pieces, LON, 0, 0, tiled=True, axis_index_groups=from_far(...  31.8 us
    all_to_all x2, blocking collectives, local(): lax.all_to_all(sums, PLANE, 0, 0, tiled=True, axis_index_groups=plane)  24.1 us
    all_to_all x1, blocking collectives, local(): lax.all_to_all(sums, 'z', 0, 0, tiled=True, axis_index_groups=from_far(de...  14.7 us
    ppermute x1, starting transfers between devices, local(): outer = lax.ppermute(outer, LAT, swap)  4.59 us
    all_gather x1, blocking collectives, local(): inner = lax.all_gather(inner, 'c', axis=0, tiled=True)  4.45 us
    pallas_call x7, Pallas kernels, call(): pl.pallas_call(kernel, name=name, out_shape=shapes[0] if single else shap...  4.42 us
  transfers between devices with their start and end apart: 1, of which 0 were waited for; matrix products, arithmetic and copies ran while one was open for 0% of the time, Pallas kernels for 1%

profile of v8, /device:TPU:1, one launch (start us, length us, event | category | flops | bytes accessed | tf_op | source)
XLA Modules:
  0.0 84.8 jit_solution(178399885172577640)
XLA Ops:
  0.6 1.1 %first.1 = (bf16[16,8192]{1,0:T(8,128)(2,1)S(1)}, bf16[288,64]{1,0:T(8,128)(2,1)S(1)}, f32[1,64]{1,0:T(1,128)S(1)}, f32[1,64]{1,0:T(1,128)S(1)}, s32[16,256]{1,0...) custom-call(s32[1]{0:T(128)} %bitcast.core_ref, ...), custom_call_target="tpu_custom_call" | custom-call | tf_op jit(solution)/shard_map/first/pallas_call | solution.py:240
  1.7 4.6 %collective-permute-start = (bf16[1,8192]{1,0:T(2,128)(2,1)S(1)}, bf16[1,8192]{1,0:T(2,128)(2,1)S(1)}, u32[]{:S(2)}, u32[]{:S(2)}) collective-permute-start(bf16[1,8192]{1,0:T(2,128)(2,1)S(1)} %get-tuple-element.33), channel_id=1, source_target_pairs={{32,64},{64,32},{96,128},{128,96},{160,192},{192,160},{224,256},{2... | collective-permute-start | bytes 49160 | tf_op jit(solution)/shard_map/ppermute | solution.py:280
  6.3 4.5 %all_gather.3.after_ref.inner_ref = f32[128,128]{1,0:T(8,128)S(1)} all-gather(f32[64,128]{1,0:T(8,128)S(1)} %get-tuple-element.34), channel_id=1, replica_groups=mesh['xh'=2,'y'=4,'c'=2,'z'=16,'xl'=2] {'c'}, dimensions={0}, use_global_device_ids=true | all-gather | bytes 98304 | tf_op jit(solution)/shard_map/all_gather | solution.py:281
  10.8 0.5 prepare.1
  11.3 0.0 collective-permute-done.outer_ref
  11.3 0.1 pack.1
  11.4 31.8 %all_to_all.20.r_ref = bf16[32,40,128]{2,1,0:T(8,128)(2,1)S(1)} all-to-all(bf16[32,40,128]{2,1,0:T(8,128)(2,1)S(1)} %pack.1), channel_id=1, replica_groups={{18,19,20,21,22,23,24,25,26,27,28,29,30,31,0,1,2,3,4,5,6,7,8,9,10,11,12..., dimensions={0} | all-to-all | bytes 655360 | tf_op jit(solution)/shard_map/all_to_all | solution.py:311
  43.3 1.9 %conv.1 = (bf16[64,8,128]{2,1,0:T(8,128)(2,1)S(1)}, f32[32,8,128]{2,1,0:T(8,128)S(1)}) custom-call(bf16[32,40,128]{2,1,0:T(8,128)(2,1)S(1)} %all_to_all.20.r_ref, bf16[128,384]{1,0:T(8,128)(2,1)S(1)} %get-tuple-element.49.w_ref, f32[64,256]{1,0:T(8,128)S(1)} %get-tuple-element.50.bias_ref, f32[64,256]{1,0:T(8,128)S(1)} %get-tuple-element.51.land_ref, ...), custom_call_target="tpu_custom_call" | custom-call | tf_op jit(solution)/shard_map/conv/pallas_call | solution.py:240
  45.1 12.5 %all_to_all.21.x_ref = f32[32,8,128]{2,1,0:T(8,128)S(1)} all-to-all(f32[32,8,128]{2,1,0:T(8,128)S(1)} %get-tuple-element.54), channel_id=1, replica_groups={{416,448,480,257,289,321,353,385,417,449,481,0,32,64,96,128,160,192,224..., dimensions={0} | all-to-all | bytes 262144 | tf_op jit(solution)/shard_map/all_to_all | solution.py:328
  57.7 14.7 %all_to_all.22.x_ref = f32[16,8,128]{2,1,0:T(8,128)S(1)} all-to-all(f32[16,8,128]{2,1,0:T(8,128)S(1)} %sum_plane.1), channel_id=1, replica_groups={{16,18,20,22,24,26,28,30,0,2,4,6,8,10,12,14},{17,19,21,23,25,27,29,31,1..., dimensions={0} | all-to-all | bytes 131072 | tf_op jit(solution)/shard_map/all_to_all | solution.py:330
  72.3 11.6 %all_to_all.23.x_ref = bf16[32,8,128]{2,1,0:T(8,128)(2,1)S(1)} all-to-all(bf16[32,8,128]{2,1,0:T(8,128)(2,1)S(1)} %sum_z.1), channel_id=1, replica_groups={{416,448,480,257,289,321,353,385,417,449,481,0,32,64,96,128,160,192,224..., dimensions={0} | all-to-all | bytes 131072 | tf_op jit(solution)/shard_map/all_to_all | solution.py:332
  84.0 0.8 unpack.1
  (2 shorter events, 0.1 us)
Async XLA Ops:
  1.7 9.5 %collective-permute-start = (bf16[1,8192]{1,0:T(2,128)(2,1)S(1)}, bf16[1,8192]{1,0:T(2,128)(2,1)S(1)}, u32[]{:S(2)}, u32[]{:S(2)}) collective-permute-start(bf16[1,8192]{1,0:T(2,128)(2,1)S(1)} %get-tuple-element.33), channel_id=1, source_target_pairs={{32,64},{64,32},{96,128},{128,96},{160,192},{192,160},{224,256},{2... | collective-permute-start | bytes 49160 | tf_op jit(solution)/shard_map/ppermute | solution.py:280
